TPU v7x, 512 devices: a whole 4x8x8 slice. The times are simulated.
512 devices in a mesh: lat: 32 (over z, y_lo), lon: 16 (over y_hi, x, core).
Axes of the slice: x: 4, y: 8 (y_hi: 2, y_lo: 4; y = y_hi * 4 + y_lo), z: 8, core: 2. Of those that a mesh axis runs over, the one named last changes fastest.
Arguments:
- state_field: bfloat16 [6, 384, 192, 192], P(None, 'lat', 'lon'), may hold values from -6 to 6
- attn_bias: bfloat16 [64, 6, 144, 144], P('lat'), may hold values from -8 to 300
- region_ids: int32 [384, 192], P('lat', 'lon'), may hold values from 0 to 3
- w_qkv: bfloat16 [192, 576], replicated, may hold values from -0.4375 to 0.4375
- w_out: bfloat16 [192, 192], replicated, may hold values from -0.4375 to 0.4375
- w_up: bfloat16 [192, 768], replicated, may hold values from -0.4375 to 0.4375
- w_down: bfloat16 [768, 192], replicated, may hold values from -0.21875 to 0.21875
Outputs:
- output: bfloat16 [6, 384, 192, 192], P(None, 'lat', 'lon')
All inputs are finite; a program needn't handle non-finite values.
Results may differ from a plain program's by a relative error of at most 0.012.
Values may be sent and summed in bfloat16 or wider, within the bound.
A program may use at most 64 MiB of HBM per device.

v0:
```python
import jax
import jax.numpy as jnp
from jax import lax
from jax.sharding import PartitionSpec as P

HEADS = 6
WZ = 2
WY = 6
WX = 12
WIN = 144


epsilon = 1e-05


def from_behind(value, axis, steps):
    count = lax.axis_size(axis)
    first, last = (max(0, -steps), min(count, count - steps))
    return lax.ppermute(value, axis, [(source, source + steps) for source in range(first, last)])


def passed_along(block, axis, distance):
    devices = range(lax.axis_size(axis))
    route = [((i - distance) % len(devices), i) for i in devices]
    return lax.ppermute(block, axis, route)


def layer_norm(values):
    average = jnp.mean(values, axis=-1, keepdims=True)
    centred = values - average
    variance = jnp.mean(centred * centred, axis=-1, keepdims=True)
    return centred * lax.rsqrt(variance + epsilon)


def shards(state_field, attn_bias, region_ids, w_qkv, w_out, w_up, w_down):
    n_lev, lat_rows, lon_cols, width = state_field.shape
    lat_half = WY // 2
    lon_half = WX // 2
    lev_blocks = n_lev // WZ
    lat_blocks = lat_rows // WY
    lon_blocks = lon_cols // WX
    head_dim = width // HEADS
    normed = layer_norm(state_field.astype(jnp.float32)).astype(jnp.bfloat16)
    normed = jnp.roll(normed, -(WZ // 2), axis=0)
    strip_below = from_behind(normed[:, :lat_half], "lat", -1)
    lat_moved = jnp.concatenate([normed[:, lat_half:], strip_below], axis=1)
    strip_right = passed_along(lat_moved[:, :, :lon_half], "lon", -1)
    shifted = jnp.concatenate([lat_moved[:, :, lon_half:], strip_right], axis=2)
    windows = shifted.reshape(lev_blocks, WZ, lat_blocks, WY, lon_blocks, WX, width)
    windows = windows.transpose(0, 2, 4, 1, 3, 5, 6).reshape(-1, width)
    projected = jnp.dot(windows, w_qkv, preferred_element_type=jnp.float32).astype(jnp.bfloat16)
    projected = projected.reshape(lev_blocks, lat_blocks, lon_blocks, WIN, 3, HEADS, head_dim)
    queries = projected[:, :, :, :, 0]
    key_vecs = projected[:, :, :, :, 1]
    value_vecs = projected[:, :, :, :, 2]
    score_scale = 1.0 / head_dim**0.5
    scores = (
        jnp.einsum("zyxqhd,zyxkhd->zyxhqk", queries, key_vecs, preferred_element_type=jnp.float32)
        * score_scale
    )
    scores = scores + attn_bias.astype(jnp.float32)[None, :, None]
    labels_win = region_ids.reshape(lat_blocks, WY, lon_blocks, WX).transpose(0, 2, 1, 3)
    labels_win = labels_win.reshape(lat_blocks, lon_blocks, WY * WX)
    labels_win = jnp.broadcast_to(labels_win[:, :, None, :], (lat_blocks, lon_blocks, WZ, WY * WX))
    labels_win = labels_win.reshape(lat_blocks, lon_blocks, WIN)
    token_pos = jnp.arange(WIN, dtype=jnp.int32)
    lat_offset = token_pos // WX % WY
    band_ids = lax.axis_index("lat") * lat_blocks + jnp.arange(lat_blocks, dtype=jnp.int32)
    band_rows = band_ids[:, None] * WY + lat_offset[None, :]
    valid_key = band_rows < lat_rows * lax.axis_size("lat") - lat_half
    allowed = (labels_win[:, :, :, None] == labels_win[:, :, None, :]) & valid_key[:, None, None, :]
    scores = jnp.where(allowed[None, :, :, None], scores, -1000000000.0)
    attn_probs = jax.nn.softmax(scores, axis=-1).astype(jnp.bfloat16)
    context = jnp.einsum(
        "zyxhqk,zyxkhd->zyxqhd", attn_probs, value_vecs, preferred_element_type=jnp.float32
    )
    context = context.astype(jnp.bfloat16).reshape(-1, width)
    mixed = jnp.dot(context, w_out, preferred_element_type=jnp.float32).astype(jnp.bfloat16)
    mixed = mixed.reshape(lev_blocks, lat_blocks, lon_blocks, WZ, WY, WX, width)
    mixed = mixed.transpose(0, 3, 1, 4, 2, 5, 6).reshape(n_lev, lat_rows, lon_cols, width)
    strip_left = passed_along(mixed[:, :, lon_cols - lon_half :], "lon", 1)
    lon_moved = jnp.concatenate([strip_left, mixed[:, :, : lon_cols - lon_half]], axis=2)
    strip_above = from_behind(lon_moved[:, lat_rows - lat_half :], "lat", 1)
    returned = jnp.concatenate([strip_above, lon_moved[:, : lat_rows - lat_half]], axis=1)
    returned = jnp.roll(returned, WZ // 2, axis=0)
    residual = state_field.astype(jnp.float32) + returned.astype(jnp.float32)
    normed_two = layer_norm(residual).astype(jnp.bfloat16)
    hidden = jax.nn.gelu(
        jnp.dot(normed_two.reshape(-1, width), w_up, preferred_element_type=jnp.float32)
    )
    hidden = hidden.astype(jnp.bfloat16)
    update = jnp.dot(hidden, w_down, preferred_element_type=jnp.float32).reshape(residual.shape)
    return (residual + update).astype(jnp.bfloat16)


def solution(mesh):
    placed = (
        P(None, "lat", "lon", None),
        P("lat", None, None, None),
        P("lat", "lon"),
        P(),
        P(),
        P(),
        P(),
    )
    return jax.shard_map(
        shards, mesh=mesh, in_specs=placed, out_specs=P(None, "lat", "lon", None), check_vma=False
    )
```

profile of v0, /device:TPU:256, one launch (start us, length us, event | category | flops | bytes accessed | tf_op | source)
XLA Modules:
  0.0 80.5 jit_solution(3798209692573322889)
XLA Ops:
  0.0 0.0 copy-start
  0.0 0.0 copy-start.1
  0.0 1.5 %convert_reduce_fusion = f32[6,12,12]{0,2,1:T(8,128)S(1)} fusion(bf16[6,12,12,192]{3,2,1,0:T(8,128)(2,1)} %param.7), kind=kLoop, calls=%fused_computation.21 | loop fusion | flops 330912 | bytes 335232 | tf_op jit(solution)/shard_map/reduce_sum | solution.py:29
  1.6 0.0 copy-done.1
  1.6 0.6 fusion.24
  2.2 0.4 fusion.25
  2.6 0.0 copy-start.6
  2.6 0.0 copy-start.3
  2.6 0.1 slice.65
  2.7 0.1 slice.64
  2.9 0.1 pad_maximum_fusion.7
  3.0 4.6 %collective-permute-start = (bf16[6,3,12,192]{3,0,2,1:T(8,128)(2,1)S(1)}, bf16[6,3,12,192]{3,0,2,1:T(8,128)(2,1)S(1)}, u32[]{:S(2)}, u32[]{:S(2)}) collective-permute-start(bf16[6,3,12,192]{3,0,2,1:T(8,128)(2,1)S(1)} %pad_maximum_fusion.7), channel_id=1, source_target_pairs={{16,0},{32,16},{48,32},{64,48},{80,64},{96,80},{112,96},{128,112},... | collective-permute-start | bytes 248840 | tf_op jit(solution)/shard_map/ppermute | solution.py:19
  7.6 0.0 copy-done.6
  7.6 0.1 broadcast_in_dim.18
  7.7 0.1 broadcast_in_dim.20
  7.8 0.0 copy-done.3
  7.8 1.6 %copy.29 = f32[2,6,144,144]{2,3,1,0:T(8,128)} copy(bf16[2,6,144,144]{3,2,1,0:T(8,128)(2,1)S(1)} %copy-done.3) | data formatting | bytes 1492992 | tf_op jit(solution)/shard_map/convert_element_type | solution.py:61
  9.4 0.1 add_compare_fusion
  9.5 0.2 fusion.30
  9.7 1.0 %collective-permute-done = bf16[6,3,12,192]{3,0,2,1:T(8,128)(2,1)S(1)} collective-permute-done((bf16[6,3,12,192]{3,0,2,1:T(8,128)(2,1)S(1)}, bf16[6,3,12,192]{3,0,2,1:T(8,128)(2,1)S(1)}, u32[]{:S(2)}, u32[]{:S(2)}) %collective-permute-start) | collective-permute-done | bytes 82976 | tf_op jit(solution)/shard_map/ppermute | solution.py:19
  10.7 0.1 fusion.31
  10.8 8.3 %collective-permute-start.1 = (bf16[6,12,6,192]{3,0,2,1:T(8,128)(2,1)S(1)}, bf16[6,12,6,192]{3,0,2,1:T(8,128)(2,1)S(1)}, u32[]{:S(2)}, u32[]{:S(2)}) collective-permute-start(bf16[6,12,6,192]{3,0,2,1:T(8,128)(2,1)S(1)} %get-tuple-element.11), channel_id=1, source_target_pairs={{1,0},{2,1},{3,2},{4,3},{5,4},{6,5},{7,6},{8,7},{9,8},{10,9},{11,1... | collective-permute-start | bytes 497672 | tf_op jit(solution)/shard_map/ppermute | solution.py:25
  19.1 0.1 compare_and_fusion
  19.2 4.2 %collective-permute-done.1 = bf16[6,12,6,192]{3,0,2,1:T(8,128)(2,1)S(1)} collective-permute-done((bf16[6,12,6,192]{3,0,2,1:T(8,128)(2,1)S(1)}, bf16[6,12,6,192]{3,0,2,1:T(8,128)(2,1)S(1)}, u32[]{:S(2)}, u32[]{:S(2)}) %collective-permute-start.1) | collective-permute-done | bytes 165920 | tf_op jit(solution)/shard_map/ppermute | solution.py:25
  23.4 0.1 pad_maximum_fusion.4
  23.6 0.4 reshape.155
  24.0 0.0 copy-start.4
  24.0 0.1 copy.60
  24.1 0.2 reshape.156
  24.3 0.6 copy-done.4
  24.9 1.5 %convolution_convert_fusion = bf16[864,576]{0,1:T(8,128)(2,1)} fusion(bf16[864,192]{1,0:T(8,128)(2,1)S(1)} %reshape.156, bf16[192,576]{1,0:T(8,128)(2,1)S(1)} %copy-done.4), kind=kOutput, calls=%fused_computation.22 | convolution fusion | flops 191600640 | bytes 1548288 | tf_op jit(solution)/shard_map/dot_general | solution.py:51
  26.4 4.7 %reshape.157 = bf16[3,2,1,144,3,6,32]{3,1,0,6,5,4,2:T(2,128)(2,1)S(1)} reshape(bf16[864,576]{0,1:T(8,128)(2,1)} %convolution_convert_fusion) | data formatting | bytes 1990656 | tf_op jit(solution)/shard_map/reshape | solution.py:52
  31.1 1.2 %fusion.39 = (bf16[3,2,1,144,1,6,32]{3,1,0,6,5,4,2:T(2,128)(2,1)S(1)}, bf16[3,2,1,144,1,6,32]{3,1,0,6,5,4,2:T(2,128)(2,1)S(1)}, bf16[3,2,1,144,1,6,32]{3,1,0,6,5,4,2:T(2,128)(2,1)S(1)}) fusion(bf16[3,2,1,144,3,6,32]{3,1,0,6,5,4,2:T(2,128)(2,1)S(1)} %reshape.157), kind=kLoop, calls=%fused_computation.79 | loop fusion | bytes 1990656 | tf_op jit(solution)/shard_map/slice | solution.py:55
  32.4 0.0 copy-start.2
  32.4 0.9 %fusion.29 = f32[3,2,6,144,144]{3,4,2,1,0:T(8,128)S(1)} fusion(bf16[3,2,1,144,1,6,32]{3,1,0,6,5,4,2:T(2,128)(2,1)S(1)} %get-tuple-element.7, bf16[3,2,1,144,1,6,32]{3,1,0,6,5,4,2:T(2,128)(2,1)S(1)} %get-tuple-element.6), kind=kOutput, calls=%fused_computation.51 | convolution fusion | flops 47775744 | bytes 3649536 | tf_op jit(solution)/shard_map/zyxqhd,zyxkhd->zyxhqk/dot_general | solution.py:58
  33.3 0.6 copy-done.2
  33.8 1.8 %fusion.41 = (f32[3,2,6,144]{3,2,1,0:T(8,128)S(1)}, f32[3,2,6,144,144]{3,4,2,1,0:T(8,128)S(1)}) fusion(f32[3,2,6,144,144]{3,4,2,1,0:T(8,128)S(1)} %fusion.29, f32[2,6,144,144]{2,3,1,0:T(8,128)S(1)} %copy-done.2, pred[2,144,144]{1,2,0:T(8,128)(4,1)S(1)} %compare_and_fusion), kind=kOutput, calls=%fused_computation.81 | output fusion | flops 5972111 | bytes 7029504 | tf_op jit(solution)/shard_map/sub | solution.py:73
  35.7 0.5 fusion.23
  36.2 0.0 copy-start.5
  36.2 0.6 copy.31
  36.8 0.3 reshape.161
  37.1 0.0 copy-done.5
  37.1 0.3 convolution_convert_fusion.1
  37.5 0.2 copy.32
  37.7 0.1 reshape.162
  37.8 0.5 copy.33
  38.3 0.4 reshape.163
  38.8 1.9 %collective-permute-start.2 = (bf16[6,12,6,192]{3,0,2,1:T(8,128)(2,1)S(1)}, bf16[6,12,6,192]{3,0,2,1:T(8,128)(2,1)S(1)}, u32[]{:S(2)}, u32[]{:S(2)}) collective-permute-start(bf16[6,12,6,192]{3,0,2,1:T(8,128)(2,1)S(1)} %get-tuple-element.8), channel_id=1, source_target_pairs={{15,0},{0,1},{1,2},{2,3},{3,4},{4,5},{5,6},{6,7},{7,8},{8,9},{9,10... | collective-permute-start | bytes 497672 | tf_op jit(solution)/shard_map/ppermute | solution.py:25
  40.7 20.0 %collective-permute-done.2 = bf16[6,12,6,192]{3,0,2,1:T(8,128)(2,1)S(1)} collective-permute-done((bf16[6,12,6,192]{3,0,2,1:T(8,128)(2,1)S(1)}, bf16[6,12,6,192]{3,0,2,1:T(8,128)(2,1)S(1)}, u32[]{:S(2)}, u32[]{:S(2)}) %collective-permute-start.2) | collective-permute-done | bytes 165920 | tf_op jit(solution)/shard_map/ppermute | solution.py:25
  60.7 2.1 %collective-permute-start.3 = (bf16[6,3,12,192]{3,0,2,1:T(8,128)(2,1)S(1)}, bf16[6,3,12,192]{3,0,2,1:T(8,128)(2,1)S(1)}, u32[]{:S(2)}, u32[]{:S(2)}) collective-permute-start(bf16[6,3,12,192]{3,0,2,1:T(8,128)(2,1)S(1)} %pad_maximum_fusion.6), channel_id=1, source_target_pairs={{0,16},{16,32},{32,48},{48,64},{64,80},{80,96},{96,112},{112,128},... | collective-permute-start | bytes 248840 | tf_op jit(solution)/shard_map/ppermute | solution.py:19
  62.8 8.8 %collective-permute-done.3 = bf16[6,3,12,192]{3,0,2,1:T(8,128)(2,1)S(1)} collective-permute-done((bf16[6,3,12,192]{3,0,2,1:T(8,128)(2,1)S(1)}, bf16[6,3,12,192]{3,0,2,1:T(8,128)(2,1)S(1)}, u32[]{:S(2)}, u32[]{:S(2)}) %collective-permute-start.3) | collective-permute-done | bytes 82976 | tf_op jit(solution)/shard_map/ppermute | solution.py:19
  71.7 0.6 fusion.27
  72.3 1.0 %multiply_reduce_fusion = f32[6,12,12]{0,2,1:T(8,128)S(1)} fusion(f32[6,12,12]{0,2,1:T(8,128)S(1)} %broadcast_multiply_fusion, bf16[6,12,12,192]{3,2,1,0:T(8,128)(2,1)S(1)} %copy-done.1, bf16[6,12,6,192]{3,0,2,1:T(8,128)(2,1)S(1)} %get-tuple-element.9, bf16[6,12,6,192]{3,0,2,1:T(8,128)(2,1)S(1)} %collective-permute-done.2, ...), kind=kLoop, calls=%fused_computation.38 | loop fusion | flops 2819232 | bytes 753408 | tf_op jit(solution)/shard_map/reduce_sum | solution.py:31
  73.4 0.8 multiply_convert_fusion
  74.2 0.0 copy-start.7
  74.2 0.1 copy.34
  74.3 0.2 reshape.164
  74.5 0.0 copy-done
  74.5 0.6 copy-done.7
  75.1 2.1 %fusion.17 = f32[864,192]{1,0:T(8,128)} fusion(bf16[768,192]{0,1:T(8,128)(2,1)S(1)} %copy-done, bf16[864,192]{1,0:T(8,128)(2,1)S(1)} %reshape.164, bf16[192,768]{1,0:T(8,128)(2,1)S(1)} %copy-done.7), kind=kOutput, calls=%fused_computation.25 | convolution fusion | flops 515579904 | bytes 1585152 | tf_op jit(solution)/shard_map/dot_general | solution.py:92
  77.2 1.3 %reshape.165 = f32[6,12,12,192]{3,2,1,0:T(8,128)S(1)} reshape(f32[864,192]{1,0:T(8,128)} %fusion.17) | data formatting | bytes 1327104 | tf_op jit(solution)/shard_map/reshape | solution.py:92
  78.5 1.1 %fusion.26 = bf16[6,12,12,192]{3,0,2,1:T(8,128)(2,1)S(1)} fusion(f32[6,12,12,192]{3,2,1,0:T(8,128)S(1)} %reshape.165, bf16[6,12,12,192]{3,2,1,0:T(8,128)(2,1)S(1)} %copy-done.1, bf16[6,12,6,192]{3,0,2,1:T(8,128)(2,1)S(1)} %get-tuple-element.9, bf16[6,12,6,192]{3,0,2,1:T(8,128)(2,1)S(1)} %collective-permute-done.2, ...), kind=kLoop, calls=%fused_computation.36 | loop fusion | flops 2654208 | bytes 1741824 | tf_op jit(solution)/shard_map/convert_element_type | solution.py:93
  79.6 0.9 %copy.37 = bf16[6,12,12,192]{3,2,1,0:T(8,128)(2,1)} copy(bf16[6,12,12,192]{3,0,2,1:T(8,128)(2,1)S(1)} %fusion.26) | data formatting | bytes 663552 | tf_op jit(solution)/shard_map/convert_element_type | solution.py:93
  (9 shorter events, 0.2 us)
Async XLA Ops:
  0.0 74.5 %copy-start = (bf16[768,192]{0,1:T(8,128)(2,1)S(1)}, bf16[768,192]{0,1:T(8,128)(2,1)}, u32[]{:S(2)}) copy-start(bf16[768,192]{0,1:T(8,128)(2,1)} %param.13) | copy-start | bytes 884740
  0.0 1.6 %copy-start.1 = (bf16[6,12,12,192]{3,2,1,0:T(8,128)(2,1)S(1)}, bf16[6,12,12,192]{3,2,1,0:T(8,128)(2,1)}, u32[]{:S(2)}) copy-start(bf16[6,12,12,192]{3,2,1,0:T(8,128)(2,1)} %param.7) | copy-start | bytes 995332
  2.6 5.0 %copy-start.6 = (s32[12,12]{1,0:T(8,128)S(1)}, s32[12,12]{1,0:T(8,128)}, u32[]{:S(2)}) copy-start(s32[12,12]{1,0:T(8,128)} %param.9) | copy-start | bytes 1732
  2.6 5.2 %copy-start.3 = (bf16[2,6,144,144]{3,2,1,0:T(8,128)(2,1)S(1)}, bf16[2,6,144,144]{3,2,1,0:T(8,128)(2,1)}, u32[]{:S(2)}) copy-start(bf16[2,6,144,144]{3,2,1,0:T(8,128)(2,1)} %param.8) | copy-start | bytes 1492996
  3.0 7.7 %collective-permute-start = (bf16[6,3,12,192]{3,0,2,1:T(8,128)(2,1)S(1)}, bf16[6,3,12,192]{3,0,2,1:T(8,128)(2,1)S(1)}, u32[]{:S(2)}, u32[]{:S(2)}) collective-permute-start(bf16[6,3,12,192]{3,0,2,1:T(8,128)(2,1)S(1)} %pad_maximum_fusion.7), channel_id=1, source_target_pairs={{16,0},{32,16},{48,32},{64,48},{80,64},{96,80},{112,96},{128,112},... | collective-permute-start | bytes 248840 | tf_op jit(solution)/shard_map/ppermute | solution.py:19
  10.8 12.6 %collective-permute-start.1 = (bf16[6,12,6,192]{3,0,2,1:T(8,128)(2,1)S(1)}, bf16[6,12,6,192]{3,0,2,1:T(8,128)(2,1)S(1)}, u32[]{:S(2)}, u32[]{:S(2)}) collective-permute-start(bf16[6,12,6,192]{3,0,2,1:T(8,128)(2,1)S(1)} %get-tuple-element.11), channel_id=1, source_target_pairs={{1,0},{2,1},{3,2},{4,3},{5,4},{6,5},{7,6},{8,7},{9,8},{10,9},{11,1... | collective-permute-start | bytes 497672 | tf_op jit(solution)/shard_map/ppermute | solution.py:25
  24.0 0.9 %copy-start.4 = (bf16[192,576]{1,0:T(8,128)(2,1)S(1)}, bf16[192,576]{1,0:T(8,128)(2,1)}, u32[]{:S(2)}) copy-start(bf16[192,576]{1,0:T(8,128)(2,1)} %param.10) | copy-start | bytes 663556
  32.4 1.5 %copy-start.2 = (f32[2,6,144,144]{2,3,1,0:T(8,128)S(1)}, f32[2,6,144,144]{2,3,1,0:T(8,128)}, u32[]{:S(2)}) copy-start(f32[2,6,144,144]{2,3,1,0:T(8,128)} %copy.29) | copy-start | bytes 2985988
  36.2 1.0 %copy-start.5 = (bf16[192,192]{1,0:T(8,128)(2,1)S(1)}, bf16[192,192]{1,0:T(8,128)(2,1)}, u32[]{:S(2)}) copy-start(bf16[192,192]{1,0:T(8,128)(2,1)} %param.11) | copy-start | bytes 221188
  38.8 21.9 %collective-permute-start.2 = (bf16[6,12,6,192]{3,0,2,1:T(8,128)(2,1)S(1)}, bf16[6,12,6,192]{3,0,2,1:T(8,128)(2,1)S(1)}, u32[]{:S(2)}, u32[]{:S(2)}) collective-permute-start(bf16[6,12,6,192]{3,0,2,1:T(8,128)(2,1)S(1)} %get-tuple-element.8), channel_id=1, source_target_pairs={{15,0},{0,1},{1,2},{2,3},{3,4},{4,5},{5,6},{6,7},{7,8},{8,9},{9,10... | collective-permute-start | bytes 497672 | tf_op jit(solution)/shard_map/ppermute | solution.py:25
  60.7 10.9 %collective-permute-start.3 = (bf16[6,3,12,192]{3,0,2,1:T(8,128)(2,1)S(1)}, bf16[6,3,12,192]{3,0,2,1:T(8,128)(2,1)S(1)}, u32[]{:S(2)}, u32[]{:S(2)}) collective-permute-start(bf16[6,3,12,192]{3,0,2,1:T(8,128)(2,1)S(1)} %pad_maximum_fusion.6), channel_id=1, source_target_pairs={{0,16},{16,32},{32,48},{48,64},{64,80},{80,96},{96,112},{112,128},... | collective-permute-start | bytes 248840 | tf_op jit(solution)/shard_map/ppermute | solution.py:19
  74.2 1.0 %copy-start.7 = (bf16[192,768]{1,0:T(8,128)(2,1)S(1)}, bf16[192,768]{1,0:T(8,128)(2,1)}, u32[]{:S(2)}) copy-start(bf16[192,768]{1,0:T(8,128)(2,1)} %param.12) | copy-start | bytes 884740
where the time goes:
time: 80.8 us; the launch traced here: 80.5 us
  waiting for transfers between devices  34 us (42%)
  starting transfers between devices  16.9 us (21%)
  local copies, waits for them, and re-layouts  15.1 us (19%)
  other arithmetic  8.81 us (11%)
  matrix products  5.28 us (7%)
    ppermute x2, waiting for transfers between devices, passed_along(): return lax.ppermute(block, axis, route)  24.2 us
    ppermute x2, starting transfers between devices, passed_along(): return lax.ppermute(block, axis, route)  10.2 us
    ppermute x2, waiting for transfers between devices, from_behind(): lax.ppermute(value, axis, [(source, source + steps) for source in range(f...  9.79 us
    ppermute x2, starting transfers between devices, from_behind(): lax.ppermute(value, axis, [(source, source + steps) for source in range(f...  6.7 us
    reshape x1, local copies, waits for them, and re-layouts, shards(): projected.reshape(lev_blocks, lat_blocks, lon_blocks, WIN, 3, HEADS, head...  4.72 us
    reduce_sum x2, other arithmetic, layer_norm(): average = jnp.mean(values, axis=-1, keepdims=True)  2.18 us
    dot_general x1, matrix products, shards(): jnp.dot(hidden, w_down, preferred_element_type=jnp.float32)  2.09 us
    sub x1, other arithmetic, shards(): attn_probs = jax.nn.softmax(scores, axis=-1).astype(jnp.bfloat16)  1.84 us
  transfers between devices with their start and end apart: 4, of which 4 were waited for; matrix products, arithmetic and copies ran while one was open for 3% of the time, Pallas kernels for 0%

commit v1 on v0

v1 whole, which is shorter than its diff:
```python
import functools

import jax
import jax.numpy as jnp
from jax import lax
from jax.experimental import pallas as pl
from jax.experimental.pallas import tpu as pltpu
from jax.sharding import PartitionSpec as P

HEADS = 6
C = 192
FF = 768
HALF = 6
NB = 72
NC = 40
BC = NB + NC
EPS = 1e-05
NEG = -1000000000.0
SCALE = 1.0 / 32**0.5
MESH = pl.DeviceIdType.MESH
F32 = jnp.float32
BF16 = jnp.bfloat16

LON = (3 * BC, 176, 160)
LAT = (128, 64, 64)
RET = (6 * NC, 128, 112)


def dot(a, b):
    return jnp.dot(a, b, preferred_element_type=F32)


def dot_nt(a, b):
    return lax.dot_general(a, b, (((1,), (1,)), ((), ())), preferred_element_type=F32)


def dot_tt(a, b):
    return lax.dot_general(a, b, (((0,), (1,)), ((), ())), preferred_element_type=F32)


def layer_norm(values):
    average = jnp.mean(values, axis=-1, keepdims=True)
    centred = values - average
    variance = jnp.mean(centred * centred, axis=-1, keepdims=True)
    return centred * lax.rsqrt(variance + EPS)


def one_hot(hit):
    return jnp.where(hit, 1.0, 0.0).astype(BF16)


def iota(shape, axis):
    return lax.broadcasted_iota(jnp.int32, shape, axis)


def by36(t):
    return (t * 57) >> 11


def by18(t):
    return (t * 57) >> 10


def by6(t):
    return (t * 43) >> 8


def gather_of(side):
    t = iota((BC + NC, 1), 0)
    is_b = t < NB
    is_a = t >= BC
    u = jnp.where(is_a, t - BC, t - NB)
    lev = jnp.where(is_b, by36(t), by18(u))
    v = jnp.where(is_b, t - 36 * lev, u - 18 * lev)
    row = by6(v)
    col = v - 6 * row + HALF * side
    row = row + jnp.where(is_b, 3, jnp.where(is_a, 0, 9))
    source = lev * 192 + row * 16 + col
    source = jnp.where(is_b | (u < 36), source, -1)
    return one_hot(iota((BC + NC, 384), 1) == source)


def scatter_of(lev, rows, full):
    d = iota((rows * 16, 1), 0)
    row, col = d >> 4, d & 15
    side = jnp.where(col >= HALF, 1, 0)
    cc = col - HALF * side
    if full:
        at = jnp.where(row < 6, lev * 36 + row * 6 + cc, NB + lev * 18 + (row - 6) * 6 + cc)
        width = BC
    else:
        at = lev * 18 + row * 6 + cc
        width = NC
    source = jnp.where(col < 12, side * width + at, -1)
    return one_hot(iota((rows * 16, 2 * width), 1) == source)


def key_place(t, band, side):
    if band == 0:
        halo = t >= NB
        u = jnp.where(halo, t - NB, t)
        lev = by36(u)
        v = u - 36 * lev
        row = by6(v)
        col = v - 6 * row
        valid = t >= 0
    else:
        halo = t >= 2 * NC
        w = jnp.where(halo, t - 2 * NC, t)
        below = w >= NC
        u = jnp.where(below, w - NC, w)
        lev = by18(u)
        v = u - 18 * lev
        row = by6(v)
        col = v - 6 * row
        row = row + jnp.where(below, 3, 0)
        valid = u < 36
    col = col + jnp.where(halo, HALF * side, HALF * (1 - side))
    return lev, row, col, valid


def pack(buf, x, form):
    tokens, rest, second = form
    buf[0:tokens, :] = x[:, 0:128].astype(BF16)
    low, high = x[0:rest, 128:192], x[second : second + rest, 128:192]
    buf[tokens : tokens + rest, :] = jnp.concatenate([low, high], axis=1).astype(BF16)


def unpack(dst, buf, form):
    tokens, rest, second = form
    dst[0:tokens, 0:128] = buf[0:tokens, :]
    tail = buf[tokens : tokens + rest, :]
    dst[0:rest, 128:192] = tail[:, 0:64]
    dst[second : second + rest, 128:192] = tail[:, 64:128]


def attend(q, k, v, bias):
    n = q.shape[0]
    head = iota((1, C), 1) >> 5
    stacked = jnp.concatenate([jnp.where(head == h, q, 0.0) for h in range(HEADS)], axis=0)
    scores = dot_nt(stacked.astype(BF16), k) * SCALE + bias
    top = jnp.max(scores, axis=-1, keepdims=True)
    weights = jnp.exp(scores - top)
    total = jnp.sum(weights, axis=-1, keepdims=True)
    mixed = dot(weights.astype(BF16), v) * (1.0 / total)
    out = jnp.where(head == 0, mixed[0:n], 0.0)
    for h in range(1, HEADS):
        out = jnp.where(head == h, mixed[h * n : (h + 1) * n], out)
    return out


def feed_forward(residual, w_up, w_down):
    normed = layer_norm(residual).astype(BF16)
    hidden = jax.nn.gelu(dot(normed, w_up)).astype(BF16)
    return (residual + dot(hidden, w_down)).astype(BF16)


def kernel(
    n_lat,
    n_lon,
    state,
    attn_bias,
    region_ids,
    w_qkv,
    w_out,
    w_up,
    w_down,
    out,
    x_in,
    bias_in,
    region,
    region_left,
    wqkv_v,
    wq,
    wk,
    wv,
    wo_v,
    wu_v,
    wd_v,
    xp,
    st,
    normed,
    normed_a,
    m_lon,
    m_lat,
    m_ret,
    r_lon,
    r_lat,
    r_diag,
    r_ret,
    own_q,
    own_k,
    own_v,
    halo_x,
    lat_x,
    diag_x,
    halo_k,
    halo_v,
    lat_q,
    lat_k,
    lat_v,
    diag_k,
    diag_v,
    bias_b,
    bias_c,
    labels,
    mix,
    mix_ret,
    ret_x,
    out_bc,
    out_a,
    load_sem,
    send_sem,
    recv_sem,
):
    la = lax.axis_index("lat")
    lo = lax.axis_index("lon")
    right = lax.rem(lo + 1, n_lon)
    left = lax.rem(lo + n_lon - 1, n_lon)
    has_above = la > 0
    has_below = la < n_lat - 1

    barrier = pltpu.get_barrier_semaphore()
    for col in (left, right):
        pl.semaphore_signal(barrier, inc=1, device_id=(la, col), device_id_type=MESH)

    @pl.when(has_above)
    def _():
        for col in (left, lo, right):
            pl.semaphore_signal(barrier, inc=1, device_id=(la - 1, col), device_id_type=MESH)

    @pl.when(has_below)
    def _():
        for col in (left, lo, right):
            pl.semaphore_signal(barrier, inc=1, device_id=(la + 1, col), device_id_type=MESH)

    loads = [
        pltpu.make_async_copy(src, dst, load_sem.at[i])
        for i, (src, dst) in enumerate(
            [
                (state, x_in),
                (w_qkv, wqkv_v),
                (attn_bias, bias_in),
                (region_ids, region),
                (w_out, wo_v),
                (w_up, wu_v),
                (w_down, wd_v),
            ]
        )
    ]
    for load in loads:
        load.start()

    xp[...] = jnp.zeros_like(xp)
    normed_a[...] = jnp.zeros_like(normed_a)
    gathers = [gather_of(0), gather_of(1)]
    loads[0].wait()
    for lev in range(6):
        xp[lev, :, 0:12, :] = x_in[(lev + 1) % 6].astype(F32)
    for z in range(3):
        tokens = xp[2 * z : 2 * z + 2].reshape(384, C).astype(BF16)
        for side in range(2):
            x = dot(gathers[side], tokens)
            st[side, z] = x
            x = layer_norm(x)
            normed[side, z * BC : (z + 1) * BC, :] = x[0:BC]
            normed_a[side, z * NC : (z + 1) * NC, :] = x[BC : BC + NC]
    for side in range(2):
        pack(m_lon.at[side], normed[side], LON)
        pack(m_lat.at[side], normed_a[side], LAT)

    n_up = jnp.where(has_above, 3, 0)
    n_down = jnp.where(has_below, 3, 0)
    pl.semaphore_wait(barrier, 2 + n_up + n_down)

    def remote(src, dst, i, device):
        return pltpu.make_async_remote_copy(
            src_ref=src,
            dst_ref=dst,
            send_sem=send_sem.at[i],
            recv_sem=recv_sem.at[i],
            device_id=device,
            device_id_type=MESH,
        )

    to_left = remote(m_lon.at[0], r_lon.at[1], 0, (la, left))
    to_right = remote(m_lon.at[1], r_lon.at[0], 1, (la, right))
    regions = remote(region_ids, region_left, 2, (la, right))
    up = remote(m_lat, r_lat, 3, (la - 1, lo))
    up_left = remote(m_lat.at[0], r_diag.at[1], 4, (la - 1, left))
    up_right = remote(m_lat.at[1], r_diag.at[0], 5, (la - 1, right))
    down = remote(m_ret, r_ret, 6, (la + 1, lo))
    to_left.start()
    to_right.start()
    regions.start()

    @pl.when(has_above)
    def _():
        up_left.start()
        up_right.start()
        up.start()

    loads[1].wait()
    wq[...] = wqkv_v[:, 0:192]
    wk[...] = wqkv_v[:, 192:384]
    wv[...] = wqkv_v[:, 384:576]
    for side in range(2):
        x = normed[side].astype(BF16)
        own_q[side] = dot(x, wq[...])
        own_k[side] = dot(x, wk[...])
        own_v[side] = dot(x, wv[...])
    loads[2].wait()
    for band, (store, n, m) in enumerate(((bias_b, NB, 2 * NB), (bias_c, 2 * NC, 4 * NC))):
        for side in range(2):
            lev, row, col, valid = key_place(iota((m, 1), 0), band, side)
            at = jnp.where(valid, lev * 72 + row * 12 + col, -1)
            select = one_hot(iota((m, 144), 1) == at)
            rows = [dot(select[0:n], bias_in[band, h]) for h in range(HEADS)]
            rows = jnp.concatenate(rows, axis=0).astype(BF16)
            store[side] = dot_nt(rows, select)

    def apply_mask(side, source):
        labels[...] = jnp.zeros_like(labels)
        labels[0:12, 0:12] = source[...].astype(F32)
        table = labels[...].astype(BF16)
        for band, (store, n, m) in enumerate(((bias_b, NB, 2 * NB), (bias_c, 2 * NC, 4 * NC))):
            _, row, col, _ = key_place(iota((m, 1), 0), band, side)
            in_row = one_hot(iota((m, 16), 1) == row + 6 * band)
            queries = dot(in_row[0:n], table)
            queries = jnp.where(iota((n, 128), 1) == col[0:n], queries, 0.0)
            queries = jnp.sum(queries, axis=1, keepdims=True)
            _, row, col, valid = key_place(iota((1, m), 1), band, side)
            keys = dot_tt(table, in_row)
            keys = jnp.where(iota((128, m), 0) == col, keys, 0.0)
            keys = jnp.sum(keys, axis=0, keepdims=True)
            valid = valid & (la * 12 + 6 * band + row < n_lat * 12 - 3)
            keys = jnp.where(valid, keys, -1.0)
            allowed = queries == keys
            for h in range(HEADS):
                part = store[side, h * n : (h + 1) * n, :]
                store[side, h * n : (h + 1) * n, :] = jnp.where(allowed, part, NEG)

    loads[3].wait()
    apply_mask(1, region)

    regions.wait_recv()
    apply_mask(0, region_left)
    to_left.wait_recv()
    to_right.wait_recv()
    for side in range(2):
        unpack(halo_x.at[side], r_lon.at[side], LON)
        x = halo_x[side]
        halo_k[side] = dot(x, wk[...])
        halo_v[side] = dot(x, wv[...])

    @pl.when(has_below)
    def _():
        up.wait_recv()
        up_left.wait_recv()
        up_right.wait_recv()

    @pl.when(jnp.logical_not(has_below))
    def _():
        r_lat[...] = jnp.zeros_like(r_lat)
        r_diag[...] = jnp.zeros_like(r_diag)

    for side in range(2):
        unpack(lat_x.at[side], r_lat.at[side], LAT)
        unpack(diag_x.at[side], r_diag.at[side], LAT)
        x = lat_x[side]
        lat_q[side] = dot(x, wq[...])
        lat_k[side] = dot(x, wk[...])
        lat_v[side] = dot(x, wv[...])
        x = diag_x[side]
        diag_k[side] = dot(x, wk[...])
        diag_v[side] = dot(x, wv[...])

    loads[4].wait()

    def windows_c(z, carry):
        a = pl.ds(pl.multiple_of(z * NC, 8), NC)
        c = pl.ds(pl.multiple_of(z * BC + NB, 8), NC)
        for side in range(2):
            q = jnp.concatenate([own_q[side, c], lat_q[side, a]], axis=0)
            k = jnp.concatenate([own_k[side, c], lat_k[side, a], halo_k[side, c], diag_k[side, a]], axis=0)
            v = jnp.concatenate([own_v[side, c], lat_v[side, a], halo_v[side, c], diag_v[side, a]], axis=0)
            context = attend(q, k.astype(BF16), v.astype(BF16), bias_c[side])
            mixed = dot(context.astype(BF16), wo_v[...]).astype(BF16).astype(F32)
            mix[z, side, NB:BC, :] = mixed[0:NC]
            mix_ret[pl.ds(pl.multiple_of((z * 2 + side) * NC, 8), NC), :] = mixed[NC : 2 * NC]
        return carry

    lax.fori_loop(0, 3, windows_c, 0)
    pack(m_ret, mix_ret[...], RET)

    @pl.when(has_below)
    def _():
        down.start()

    def windows_b(z, carry):
        b = pl.ds(pl.multiple_of(z * BC, 8), NB)
        for side in range(2):
            k = jnp.concatenate([own_k[side, b], halo_k[side, b]], axis=0)
            v = jnp.concatenate([own_v[side, b], halo_v[side, b]], axis=0)
            context = attend(own_q[side, b], k.astype(BF16), v.astype(BF16), bias_b[side])
            mix[z, side, 0:NB, :] = dot(context.astype(BF16), wo_v[...]).astype(BF16).astype(F32)
        return carry

    lax.fori_loop(0, 3, windows_b, 0)
    loads[5].wait()
    loads[6].wait()

    for z in range(3):
        residual = jnp.concatenate([st[0, z, 0:BC] + mix[z, 0], st[1, z, 0:BC] + mix[z, 1]], axis=0)
        out_bc[...] = feed_forward(residual, wu_v[...], wd_v[...])
        for lev in range(2):
            grid = dot(scatter_of(lev, 9, True), out_bc[...]).reshape(9, 16, C)
            out[(2 * z + lev + 1) % 6, 3:12] = grid[:, 0:12, :].astype(BF16)

    @pl.when(has_above)
    def _():
        down.wait_recv()

    @pl.when(jnp.logical_not(has_above))
    def _():
        r_ret[...] = jnp.zeros_like(r_ret)

    unpack(ret_x, r_ret, RET)
    parts = [st[side, z, BC : BC + NC] for z in range(3) for side in range(2)]
    residual = jnp.concatenate(parts, axis=0) + ret_x[...].astype(F32)
    out_a[...] = feed_forward(residual, wu_v[...], wd_v[...])
    for z in range(3):
        for lev in range(2):
            grid = dot(scatter_of(lev, 3, False), out_a[z * 2 * NC : (z + 1) * 2 * NC, :]).reshape(3, 16, C)
            out[(2 * z + lev + 1) % 6, 0:3] = grid[:, 0:12, :].astype(BF16)

    to_left.wait_send()
    to_right.wait_send()
    regions.wait_send()

    @pl.when(has_above)
    def _():
        up_left.wait_send()
        up_right.wait_send()
        up.wait_send()

    @pl.when(has_below)
    def _():
        down.wait_send()


def shards(n_lat, n_lon, *args):
    def packed(form, *lead):
        return pltpu.VMEM((*lead, form[0] + form[1], 128), BF16)

    scratch = [
        pltpu.VMEM((6, 12, 12, C), BF16),
        pltpu.VMEM((2, HEADS, 144, 144), BF16),
        pltpu.VMEM((12, 12), jnp.int32),
        pltpu.VMEM((12, 12), jnp.int32),
        pltpu.VMEM((C, 3 * C), BF16),
        pltpu.VMEM((C, C), BF16),
        pltpu.VMEM((C, C), BF16),
        pltpu.VMEM((C, C), BF16),
        pltpu.VMEM((C, C), BF16),
        pltpu.VMEM((C, FF), BF16),
        pltpu.VMEM((FF, C), BF16),
        pltpu.VMEM((6, 12, 16, C), F32),
        pltpu.VMEM((2, 3, BC + NC, C), F32),
        pltpu.VMEM((2, 3 * BC, C), F32),
        pltpu.VMEM((2, 128, C), F32),
        packed(LON, 2),
        packed(LAT, 2),
        packed(RET),
        packed(LON, 2),
        packed(LAT, 2),
        packed(LAT, 2),
        packed(RET),
        pltpu.VMEM((2, 3 * BC, C), F32),
        pltpu.VMEM((2, 3 * BC, C), F32),
        pltpu.VMEM((2, 3 * BC, C), F32),
        pltpu.VMEM((2, 3 * BC, C), BF16),
        pltpu.VMEM((2, 128, C), BF16),
        pltpu.VMEM((2, 128, C), BF16),
        pltpu.VMEM((2, 3 * BC, C), F32),
        pltpu.VMEM((2, 3 * BC, C), F32),
        pltpu.VMEM((2, 128, C), F32),
        pltpu.VMEM((2, 128, C), F32),
        pltpu.VMEM((2, 128, C), F32),
        pltpu.VMEM((2, 128, C), F32),
        pltpu.VMEM((2, 128, C), F32),
        pltpu.VMEM((2, HEADS * NB, 2 * NB), F32),
        pltpu.VMEM((2, HEADS * 2 * NC, 4 * NC), F32),
        pltpu.VMEM((16, 128), F32),
        pltpu.VMEM((3, 2, BC, C), F32),
        pltpu.VMEM((6 * NC, C), F32),
        pltpu.VMEM((6 * NC, C), BF16),
        pltpu.VMEM((2 * BC, C), BF16),
        pltpu.VMEM((6 * NC, C), BF16),
        pltpu.SemaphoreType.DMA((7,)),
        pltpu.SemaphoreType.DMA((7,)),
        pltpu.SemaphoreType.DMA((7,)),
    ]
    return pl.pallas_call(
        functools.partial(kernel, n_lat, n_lon),
        out_shape=jax.ShapeDtypeStruct((6, 12, 12, C), BF16),
        in_specs=[pl.BlockSpec(memory_space=pltpu.HBM)] * 7,
        out_specs=pl.BlockSpec(memory_space=pltpu.VMEM),
        scratch_shapes=scratch,
        compiler_params=pltpu.CompilerParams(
            collective_id=0, has_side_effects=True, vmem_limit_bytes=40 * 1024 * 1024
        ),
    )(*args)


def solution(mesh):
    placed = (
        P(None, "lat", "lon", None),
        P("lat", None, None, None),
        P("lat", "lon"),
        P(),
        P(),
        P(),
        P(),
    )
    return jax.shard_map(
        functools.partial(shards, mesh.shape["lat"], mesh.shape["lon"]),
        mesh=mesh,
        in_specs=placed,
        out_specs=P(None, "lat", "lon", None),
        check_vma=False,
    )
```

time: 80.8 us -> 33.3 us (0.41)
  waiting for transfers between devices: 34 us -> 0 us
  Pallas kernels: 0 us -> 27.2 us
  starting transfers between devices: 16.9 us -> 0 us
  local copies, waits for them, and re-layouts: 15.1 us -> 5.79 us
  other arithmetic: 8.81 us -> 0 us
  matrix products: 5.28 us -> 0 us
    ppermute x4 -> x0, waiting for transfers between devices: 34 us -> none  [the longest x2 24.2 us: passed_along(): return lax.ppermute(block, axis, route)]
    pallas_call x0 -> x1, Pallas kernels: none -> 27.2 us  [shards(): pl.pallas_call(functools.partial(kernel, n_lat, n_lon), out_shape=jax.Sha...]
    ppermute x4 -> x0, starting transfers between devices: 16.9 us -> none  [the longest x2 10.2 us: passed_along(): return lax.ppermute(block, axis, route)]
    reshape x9 -> x0, local copies, waits for them, and re-layouts: 7.77 us -> none  [the longest x1 4.72 us: shards(): projected.reshape(lev_blocks, lat_blocks, lon_blocks, WIN, 3, HEADS, head...]
    dot_general x5 -> x0, matrix products: 5.28 us -> none  [the longest x1 2.09 us: shards(): jnp.dot(hidden, w_down, preferred_element_type=jnp.float32)]
    unnamed x16 -> x14, local copies, waits for them, and re-layouts: 1.81 us -> 5.79 us
    reduce_sum x4 -> x0, other arithmetic: 3.76 us -> none  [the longest x2 2.18 us: layer_norm(): average = jnp.mean(values, axis=-1, keepdims=True)]
    convert_element_type x5 -> x0, local copies, waits for them, and re-layouts: 3.41 us -> none  [the longest x1 1.58 us: shards(): scores = scores + attn_bias.astype(jnp.float32)[None, :, None]]
  transfers between devices with their start and end apart: 4 -> 0, of which waited for: 4 -> 0; matrix products, arithmetic and copies ran while one was open for 3% -> 0% of each run, Pallas kernels for 0% -> 0%
where the time goes in v1:
time: 33.3 us; the launch traced here: 33 us
  Pallas kernels  27.2 us (82%)
  local copies, waits for them, and re-layouts  5.79 us (17%)
    pallas_call x1, Pallas kernels, shards(): pl.pallas_call(functools.partial(kernel, n_lat, n_lon), out_shape=jax.Sha...  27.2 us
    unnamed x14, local copies, waits for them, and re-layouts  5.79 us

profile of v1, /device:TPU:256, one launch (start us, length us, event | category | flops | bytes accessed | tf_op | source)
XLA Modules:
  0.0 33.0 jit_solution(14323599171045190684)
XLA Ops:
  0.0 0.0 copy-start.4
  0.0 0.0 copy-start.1
  0.0 1.2 %copy.8.w_down = bf16[768,192]{1,0:T(8,128)(2,1)S(1)} copy(bf16[768,192]{0,1:T(8,128)(2,1)} %param.13) | data formatting | bytes 589824 | tf_op args[6]
  1.2 0.0 copy-done.4
  1.2 0.0 copy-done.1
  1.2 0.0 copy-start
  1.2 1.2 %copy-done = bf16[2,6,144,144]{3,2,1,0:T(8,128)(2,1)S(1)} copy-done((bf16[2,6,144,144]{3,2,1,0:T(8,128)(2,1)S(1)}, bf16[2,6,144,144]{3,2,1,0:T(8,128)(2,1)}, u32[]{:S(2)}) %copy-start) | copy-done | bytes 497688
  2.4 0.0 copy-start.2
  2.4 1.0 %copy-done.2 = bf16[192,768]{1,0:T(8,128)(2,1)S(1)} copy-done((bf16[192,768]{1,0:T(8,128)(2,1)S(1)}, bf16[192,768]{1,0:T(8,128)(2,1)}, u32[]{:S(2)}) %copy-start.2) | copy-done | bytes 294936
  3.4 0.0 copy-start.3
  3.4 0.9 %copy-done.3 = bf16[192,576]{1,0:T(8,128)(2,1)S(1)} copy-done((bf16[192,576]{1,0:T(8,128)(2,1)S(1)}, bf16[192,576]{1,0:T(8,128)(2,1)}, u32[]{:S(2)}) %copy-start.3) | copy-done | bytes 221208
  4.3 0.0 copy-start.5
  4.3 0.7 %copy-done.5 = s32[12,12]{1,0:T(8,128)S(1)} copy-done((s32[12,12]{1,0:T(8,128)S(1)}, s32[12,12]{1,0:T(8,128)}, u32[]{:S(2)}) %copy-start.5) | copy-done | bytes 600
  5.0 27.2 %shard_map.73 = bf16[6,12,12,192]{3,2,1,0:T(8,128)(2,1)S(1)} custom-call(bf16[6,12,12,192]{3,2,1,0:T(8,128)(2,1)S(1)} %copy-done.1, bf16[2,6,144,144]{3,2,1,0:T(8,128)(2,1)S(1)} %copy-done, s32[12,12]{1,0:T(8,128)S(1)} %copy-done.5, bf16[192,576]{1,0:T(8,128)(2,1)S(1)} %copy-done.3, bf16[192,192]{1,0:T(8,128)(2,1)S(1)} %copy-done.4, ...), custom_call_target="tpu_custom_call" | custom-call | tf_op jit(solution)/shard_map/pallas_call | solution.py:504
  32.2 0.8 %copy.10 = bf16[6,12,12,192]{3,2,1,0:T(8,128)(2,1)} copy(bf16[6,12,12,192]{3,2,1,0:T(8,128)(2,1)S(1)} %shard_map.73) | data formatting | bytes 663552
Async XLA Ops:
  0.0 1.2 %copy-start.4 = (bf16[192,192]{1,0:T(8,128)(2,1)S(1)}, bf16[192,192]{1,0:T(8,128)(2,1)}, u32[]{:S(2)}) copy-start(bf16[192,192]{1,0:T(8,128)(2,1)} %w_out.1) | copy-start | bytes 221188
  0.0 1.2 %copy-start.1 = (bf16[6,12,12,192]{3,2,1,0:T(8,128)(2,1)S(1)}, bf16[6,12,12,192]{3,2,1,0:T(8,128)(2,1)}, u32[]{:S(2)}) copy-start(bf16[6,12,12,192]{3,2,1,0:T(8,128)(2,1)} %state.1) | copy-start | bytes 995332
  1.2 1.2 %copy-start = (bf16[2,6,144,144]{3,2,1,0:T(8,128)(2,1)S(1)}, bf16[2,6,144,144]{3,2,1,0:T(8,128)(2,1)}, u32[]{:S(2)}) copy-start(bf16[2,6,144,144]{3,2,1,0:T(8,128)(2,1)} %attn_bias.1) | copy-start | bytes 1492996
  2.4 1.0 %copy-start.2 = (bf16[192,768]{1,0:T(8,128)(2,1)S(1)}, bf16[192,768]{1,0:T(8,128)(2,1)}, u32[]{:S(2)}) copy-start(bf16[192,768]{1,0:T(8,128)(2,1)} %w_up.1) | copy-start | bytes 884740
  3.4 0.9 %copy-start.3 = (bf16[192,576]{1,0:T(8,128)(2,1)S(1)}, bf16[192,576]{1,0:T(8,128)(2,1)}, u32[]{:S(2)}) copy-start(bf16[192,576]{1,0:T(8,128)(2,1)} %w_qkv.1) | copy-start | bytes 663556
  4.3 0.7 %copy-start.5 = (s32[12,12]{1,0:T(8,128)S(1)}, s32[12,12]{1,0:T(8,128)}, u32[]{:S(2)}) copy-start(s32[12,12]{1,0:T(8,128)} %region_ids.1) | copy-start | bytes 1732

commit v2 on v1

--- a/solution.py
+++ b/solution.py
@@ -152,7 +152,7 @@
 def feed_forward(residual, w_up, w_down):
     normed = layer_norm(residual).astype(BF16)
     hidden = jax.nn.gelu(dot(normed, w_up)).astype(BF16)
-    return (residual + dot(hidden, w_down)).astype(BF16)
+    return (residual + dot_nt(hidden, w_down)).astype(BF16)
 
 
 def kernel(
@@ -450,6 +450,8 @@
 
 
 def shards(n_lat, n_lon, *args):
+    args = (*args[:6], args[6].T)
+    args = [pltpu.with_memory_space_constraint(a, pltpu.HBM) for a in args]
     def packed(form, *lead):
         return pltpu.VMEM((*lead, form[0] + form[1], 128), BF16)
 
@@ -464,7 +466,7 @@
         pltpu.VMEM((C, C), BF16),
         pltpu.VMEM((C, C), BF16),
         pltpu.VMEM((C, FF), BF16),
-        pltpu.VMEM((FF, C), BF16),
+        pltpu.VMEM((C, FF), BF16),
         pltpu.VMEM((6, 12, 16, C), F32),
         pltpu.VMEM((2, 3, BC + NC, C), F32),
         pltpu.VMEM((2, 3 * BC, C), F32),
@@ -503,7 +505,7 @@
     ]
     return pl.pallas_call(
         functools.partial(kernel, n_lat, n_lon),
-        out_shape=jax.ShapeDtypeStruct((6, 12, 12, C), BF16),
+        out_shape=pltpu.VMEM((6, 12, 12, C), BF16),
         in_specs=[pl.BlockSpec(memory_space=pltpu.HBM)] * 7,
         out_specs=pl.BlockSpec(memory_space=pltpu.VMEM),
         scratch_shapes=scratch,

time: 33.3 us -> 28.2 us (0.85)
  local copies, waits for them, and re-layouts: 5.79 us -> 0.82 us
    unnamed x14 -> x1, local copies, waits for them, and re-layouts: 5.79 us -> 0.82 us
where the time goes in v2:
time: 28.2 us; the launch traced here: 28 us
  Pallas kernels  27.2 us (96%)
  local copies, waits for them, and re-layouts  0.82 us (3%)
    pallas_call x1, Pallas kernels, shards(): pl.pallas_call(functools.partial(kernel, n_lat, n_lon), out_shape=pltpu.V...  27.2 us
    unnamed x1, local copies, waits for them, and re-layouts  0.82 us

profile of v2, /device:TPU:256, one launch (start us, length us, event | category | flops | bytes accessed | tf_op | source)
XLA Modules:
  0.0 28.0 jit_solution(2122084328094345135)
XLA Ops:
  0.0 27.2 %shard_map.73 = bf16[6,12,12,192]{3,2,1,0:T(8,128)(2,1)S(1)} custom-call(bf16[6,12,12,192]{3,2,1,0:T(8,128)(2,1)} %state.1, bf16[2,6,144,144]{3,2,1,0:T(8,128)(2,1)} %attn_bias.1, s32[12,12]{1,0:T(8,128)} %region_ids.1, bf16[192,576]{1,0:T(8,128)(2,1)} %w_qkv.1, bf16[192,192]{1,0:T(8,128)(2,1)} %w_out.1, bf16[192,768]{1,0:T(8,128)(2,1)} %w_up.1, ...), custom_call_target="tpu_custom_call" | custom-call | tf_op jit(solution)/shard_map/pallas_call | solution.py:506
  27.2 0.8 %copy.9 = bf16[6,12,12,192]{3,2,1,0:T(8,128)(2,1)} copy(bf16[6,12,12,192]{3,2,1,0:T(8,128)(2,1)S(1)} %shard_map.73) | data formatting | bytes 663552

commit v3 on v2

--- a/solution.py
+++ b/solution.py
@@ -23,7 +23,6 @@
 
 LON = (3 * BC, 176, 160)
 LAT = (128, 64, 64)
-RET = (6 * NC, 128, 112)
 
 
 def dot(a, b):
@@ -36,6 +35,10 @@
 
 def dot_tt(a, b):
     return lax.dot_general(a, b, (((0,), (1,)), ((), ())), preferred_element_type=F32)
+
+
+def dot_tn(a, b):
+    return lax.dot_general(a, b, (((0,), (0,)), ((), ())), preferred_element_type=F32)
 
 
 def layer_norm(values):
@@ -152,7 +155,7 @@
 def feed_forward(residual, w_up, w_down):
     normed = layer_norm(residual).astype(BF16)
     hidden = jax.nn.gelu(dot(normed, w_up)).astype(BF16)
-    return (residual + dot_nt(hidden, w_down)).astype(BF16)
+    return residual + dot_nt(hidden, w_down)
 
 
 def kernel(
@@ -212,6 +215,7 @@
     load_sem,
     send_sem,
     recv_sem,
+    here_sem,
 ):
     la = lax.axis_index("lat")
     lo = lax.axis_index("lon")
@@ -219,20 +223,27 @@
     left = lax.rem(lo + n_lon - 1, n_lon)
     has_above = la > 0
     has_below = la < n_lat - 1
+    half = n_lon // 2
+    far_left = lax.rem(lo, half) == 0
+    far_right = lax.rem(lo + 1, half) == 0
+    end = far_left | far_right
+    end_on_left = lax.rem(lo + half - 1, half) == 0
+    end_on_right = lax.rem(lo + 2, half) == 0
+    mate = end_on_left | end_on_right
+    near = jnp.where(far_left, right, jnp.where(far_right, left, lo))
+    sides = ((far_left, left), (far_right, right))
 
     barrier = pltpu.get_barrier_semaphore()
-    for col in (left, right):
-        pl.semaphore_signal(barrier, inc=1, device_id=(la, col), device_id_type=MESH)
-
-    @pl.when(has_above)
-    def _():
-        for col in (left, lo, right):
-            pl.semaphore_signal(barrier, inc=1, device_id=(la - 1, col), device_id_type=MESH)
-
-    @pl.when(has_below)
-    def _():
-        for col in (left, lo, right):
-            pl.semaphore_signal(barrier, inc=1, device_id=(la + 1, col), device_id_type=MESH)
+
+    def greet(row, col):
+        pl.semaphore_signal(barrier, inc=1, device_id=(row, col), device_id_type=MESH)
+
+    pl.when(jnp.logical_not(end_on_left))(functools.partial(greet, la, left))
+    pl.when(jnp.logical_not(end_on_right))(functools.partial(greet, la, right))
+    for there, row in ((has_above, la - 1), (has_below, la + 1)):
+        pl.when(there)(functools.partial(greet, row, near))
+        for far, col in sides:
+            pl.when(there & far)(functools.partial(greet, row, col))
 
     loads = [
         pltpu.make_async_copy(src, dst, load_sem.at[i])
@@ -253,6 +264,7 @@
 
     xp[...] = jnp.zeros_like(xp)
     normed_a[...] = jnp.zeros_like(normed_a)
+    mix_ret[...] = jnp.zeros_like(mix_ret)
     gathers = [gather_of(0), gather_of(1)]
     loads[0].wait()
     for lev in range(6):
@@ -269,10 +281,6 @@
         pack(m_lon.at[side], normed[side], LON)
         pack(m_lat.at[side], normed_a[side], LAT)
 
-    n_up = jnp.where(has_above, 3, 0)
-    n_down = jnp.where(has_below, 3, 0)
-    pl.semaphore_wait(barrier, 2 + n_up + n_down)
-
     def remote(src, dst, i, device):
         return pltpu.make_async_remote_copy(
             src_ref=src,
@@ -283,41 +291,64 @@
             device_id_type=MESH,
         )
 
-    to_left = remote(m_lon.at[0], r_lon.at[1], 0, (la, left))
-    to_right = remote(m_lon.at[1], r_lon.at[0], 1, (la, right))
-    regions = remote(region_ids, region_left, 2, (la, right))
-    up = remote(m_lat, r_lat, 3, (la - 1, lo))
-    up_left = remote(m_lat.at[0], r_diag.at[1], 4, (la - 1, left))
-    up_right = remote(m_lat.at[1], r_diag.at[0], 5, (la - 1, right))
-    down = remote(m_ret, r_ret, 6, (la + 1, lo))
-    to_left.start()
-    to_right.start()
-    regions.start()
-
-    @pl.when(has_above)
-    def _():
-        up_left.start()
-        up_right.start()
-        up.start()
-
-    loads[1].wait()
-    wq[...] = wqkv_v[:, 0:192]
-    wk[...] = wqkv_v[:, 192:384]
-    wv[...] = wqkv_v[:, 384:576]
-    for side in range(2):
-        x = normed[side].astype(BF16)
-        own_q[side] = dot(x, wq[...])
-        own_k[side] = dot(x, wk[...])
-        own_v[side] = dot(x, wv[...])
-    loads[2].wait()
-    for band, (store, n, m) in enumerate(((bias_b, NB, 2 * NB), (bias_c, 2 * NC, 4 * NC))):
+    def along(side, col):
+        return remote(m_lon.at[side], r_lon.at[1 - side], 1 - side, (la, col))
+
+    def corner(side, source, row, col):
+        return remote(source.at[side], r_diag.at[1 - side], 3 - side, (row, col))
+
+    regions = remote(region_ids, region_left, 4, (la, right))
+    up = remote(m_lat, r_lat, 5, (la - 1, lo))
+
+    rows = jnp.where(has_above, 1, 0) + jnp.where(has_below, 1, 0)
+
+    def send_near():
+        @pl.when(jnp.logical_not(end))
+        def _():
+            pl.semaphore_wait(barrier, 2 + rows * jnp.where(mate, 2, 1))
+
+        @pl.when(mate)
+        def _():
+            col = jnp.where(end_on_left, left, right)
+            pl.semaphore_signal(here_sem, inc=1, device_id=(la, col), device_id_type=MESH)
+
+        @pl.when(end)
+        def _():
+            pl.semaphore_wait(here_sem, 1)
+
+        pl.when(has_above)(up.start)
+        pl.when(jnp.logical_not(far_right))(regions.start)
+        for side, (far, col) in enumerate(sides):
+            pl.when(jnp.logical_not(far))(along(side, col).start)
+
+    def send_far():
+        pl.semaphore_wait(barrier, 1 + rows)
+        pl.when(far_right)(regions.start)
+        for side, (far, col) in enumerate(sides):
+            pl.when(far & has_above)(corner(side, m_lat, la - 1, col).start)
+            pl.when(far)(along(side, col).start)
+
+    def prepare():
+        loads[1].wait()
+        wq[...] = wqkv_v[:, 0:192]
+        wk[...] = wqkv_v[:, 192:384]
+        wv[...] = wqkv_v[:, 384:576]
         for side in range(2):
-            lev, row, col, valid = key_place(iota((m, 1), 0), band, side)
-            at = jnp.where(valid, lev * 72 + row * 12 + col, -1)
-            select = one_hot(iota((m, 144), 1) == at)
-            rows = [dot(select[0:n], bias_in[band, h]) for h in range(HEADS)]
-            rows = jnp.concatenate(rows, axis=0).astype(BF16)
-            store[side] = dot_nt(rows, select)
+            x = normed[side].astype(BF16)
+            own_q[side] = dot(x, wq[...])
+            own_k[side] = dot(x, wk[...])
+            own_v[side] = dot(x, wv[...])
+        loads[2].wait()
+        for band, (store, n, m) in enumerate(((bias_b, NB, 2 * NB), (bias_c, 2 * NC, 4 * NC))):
+            for side in range(2):
+                lev, row, col, valid = key_place(iota((m, 1), 0), band, side)
+                at = jnp.where(valid, lev * 72 + row * 12 + col, -1)
+                select = one_hot(iota((m, 144), 1) == at)
+                rows = [dot(select[0:n], bias_in[band, h]) for h in range(HEADS)]
+                rows = jnp.concatenate(rows, axis=0).astype(BF16)
+                store[side] = dot_nt(rows, select)
+        loads[3].wait()
+        apply_mask(1, region)
 
     def apply_mask(side, source):
         labels[...] = jnp.zeros_like(labels)
@@ -340,24 +371,20 @@
                 part = store[side, h * n : (h + 1) * n, :]
                 store[side, h * n : (h + 1) * n, :] = jnp.where(allowed, part, NEG)
 
-    loads[3].wait()
-    apply_mask(1, region)
-
-    regions.wait_recv()
-    apply_mask(0, region_left)
-    to_left.wait_recv()
-    to_right.wait_recv()
-    for side in range(2):
-        unpack(halo_x.at[side], r_lon.at[side], LON)
-        x = halo_x[side]
-        halo_k[side] = dot(x, wk[...])
-        halo_v[side] = dot(x, wv[...])
+    def start(i, carry):
+        far_first = lo >= half
+        pl.when(i == jnp.where(far_first, 1, 0))(send_near)
+        pl.when(end & (i == jnp.where(far_first, 0, 2)))(send_far)
+        pl.when(i == jnp.where(far_first, 2, 1))(prepare)
+        return carry
+
+    lax.fori_loop(0, 3, start, 0)
 
     @pl.when(has_below)
     def _():
         up.wait_recv()
-        up_left.wait_recv()
-        up_right.wait_recv()
+        for side, (far, col) in enumerate(sides):
+            pl.when(jnp.logical_not(far))(corner(side, r_lat, la, col).start)
 
     @pl.when(jnp.logical_not(has_below))
     def _():
@@ -366,87 +393,112 @@
 
     for side in range(2):
         unpack(lat_x.at[side], r_lat.at[side], LAT)
-        unpack(diag_x.at[side], r_diag.at[side], LAT)
         x = lat_x[side]
         lat_q[side] = dot(x, wq[...])
         lat_k[side] = dot(x, wk[...])
         lat_v[side] = dot(x, wv[...])
-        x = diag_x[side]
-        diag_k[side] = dot(x, wk[...])
-        diag_v[side] = dot(x, wv[...])
-
     loads[4].wait()
-
-    def windows_c(z, carry):
-        a = pl.ds(pl.multiple_of(z * NC, 8), NC)
-        c = pl.ds(pl.multiple_of(z * BC + NB, 8), NC)
-        for side in range(2):
+    loads[5].wait()
+    loads[6].wait()
+
+    def window_column(i, carry):
+        side = jnp.where(far_left, 1 - i, i)
+
+        @pl.when(side == 0)
+        def _():
+            regions.wait_recv()
+            apply_mask(0, region_left)
+
+        along(1 - side, left).wait_recv()
+        unpack(halo_x, r_lon.at[side], LON)
+        x = halo_x[...]
+        halo_k[...] = dot(x, wk[...])
+        halo_v[...] = dot(x, wv[...])
+
+        @pl.when(has_below)
+        def _():
+            corner(1 - side, r_lat, la, left).wait_recv()
+
+        unpack(diag_x, r_diag.at[side], LAT)
+        x = diag_x[...]
+        diag_k[...] = dot(x, wk[...])
+        diag_v[...] = dot(x, wv[...])
+
+        for z in range(3):
+            a = pl.ds(z * NC, NC)
+            c = pl.ds(z * BC + NB, NC)
             q = jnp.concatenate([own_q[side, c], lat_q[side, a]], axis=0)
-            k = jnp.concatenate([own_k[side, c], lat_k[side, a], halo_k[side, c], diag_k[side, a]], axis=0)
-            v = jnp.concatenate([own_v[side, c], lat_v[side, a], halo_v[side, c], diag_v[side, a]], axis=0)
+            k = jnp.concatenate([own_k[side, c], lat_k[side, a], halo_k[c], diag_k[a]], axis=0)
+            v = jnp.concatenate([own_v[side, c], lat_v[side, a], halo_v[c], diag_v[a]], axis=0)
             context = attend(q, k.astype(BF16), v.astype(BF16), bias_c[side])
             mixed = dot(context.astype(BF16), wo_v[...]).astype(BF16).astype(F32)
-            mix[z, side, NB:BC, :] = mixed[0:NC]
-            mix_ret[pl.ds(pl.multiple_of((z * 2 + side) * NC, 8), NC), :] = mixed[NC : 2 * NC]
+            mix[z * BC + NB : (z + 1) * BC, :] = mixed[0:NC]
+            mix_ret[z * NC : (z + 1) * NC, :] = mixed[NC : 2 * NC]
+        pack(m_ret.at[side], mix_ret[...], LAT)
+
+        @pl.when(has_below)
+        def _():
+            down(side).start()
+
+        for z in range(3):
+            b = pl.ds(z * BC, NB)
+            k = jnp.concatenate([own_k[side, b], halo_k[b]], axis=0)
+            v = jnp.concatenate([own_v[side, b], halo_v[b]], axis=0)
+            context = attend(own_q[side, b], k.astype(BF16), v.astype(BF16), bias_b[side])
+            mix[z * BC : z * BC + NB, :] = dot(context.astype(BF16), wo_v[...]).astype(BF16).astype(F32)
+        residual = jnp.concatenate([st[side, z, 0:BC] for z in range(3)], axis=0) + mix[...]
+        out_bc[side] = feed_forward(residual, wu_v[...], wd_v[...]).astype(BF16)
         return carry
 
-    lax.fori_loop(0, 3, windows_c, 0)
-    pack(m_ret, mix_ret[...], RET)
-
-    @pl.when(has_below)
-    def _():
-        down.start()
-
-    def windows_b(z, carry):
-        b = pl.ds(pl.multiple_of(z * BC, 8), NB)
-        for side in range(2):
-            k = jnp.concatenate([own_k[side, b], halo_k[side, b]], axis=0)
-            v = jnp.concatenate([own_v[side, b], halo_v[side, b]], axis=0)
-            context = attend(own_q[side, b], k.astype(BF16), v.astype(BF16), bias_b[side])
-            mix[z, side, 0:NB, :] = dot(context.astype(BF16), wo_v[...]).astype(BF16).astype(F32)
-        return carry
-
-    lax.fori_loop(0, 3, windows_b, 0)
-    loads[5].wait()
-    loads[6].wait()
-
-    for z in range(3):
-        residual = jnp.concatenate([st[0, z, 0:BC] + mix[z, 0], st[1, z, 0:BC] + mix[z, 1]], axis=0)
-        out_bc[...] = feed_forward(residual, wu_v[...], wd_v[...])
-        for lev in range(2):
-            grid = dot(scatter_of(lev, 9, True), out_bc[...]).reshape(9, 16, C)
+    def down(side):
+        return remote(m_ret.at[side], r_ret.at[side], 6 + side, (la + 1, lo))
+
+    lax.fori_loop(0, 2, window_column, 0)
+
+    for lev in range(2):
+        scatter = scatter_of(lev, 9, True)
+        for z in range(3):
+            part = pl.ds(z * BC, BC)
+            grid = dot(scatter, jnp.concatenate([out_bc[0, part], out_bc[1, part]], axis=0)).reshape(9, 16, C)
             out[(2 * z + lev + 1) % 6, 3:12] = grid[:, 0:12, :].astype(BF16)
 
     @pl.when(has_above)
     def _():
-        down.wait_recv()
+        down(0).wait_recv()
+        down(1).wait_recv()
 
     @pl.when(jnp.logical_not(has_above))
     def _():
         r_ret[...] = jnp.zeros_like(r_ret)
 
-    unpack(ret_x, r_ret, RET)
-    parts = [st[side, z, BC : BC + NC] for z in range(3) for side in range(2)]
-    residual = jnp.concatenate(parts, axis=0) + ret_x[...].astype(F32)
-    out_a[...] = feed_forward(residual, wu_v[...], wd_v[...])
-    for z in range(3):
-        for lev in range(2):
-            grid = dot(scatter_of(lev, 3, False), out_a[z * 2 * NC : (z + 1) * 2 * NC, :]).reshape(3, 16, C)
+    for side in range(2):
+        unpack(ret_x.at[side], r_ret.at[side], LAT)
+    residual = [
+        st[side, z, BC : BC + NC] + ret_x[side, z * NC : (z + 1) * NC, :].astype(F32) for z in range(3) for side in range(2)
+    ]
+    out_a[...] = feed_forward(jnp.concatenate(residual, axis=0), wu_v[...], wd_v[...]).astype(BF16)
+    for lev in range(2):
+        scatter = scatter_of(lev, 3, False)
+        for z in range(3):
+            grid = dot(scatter, out_a[z * 2 * NC : (z + 1) * 2 * NC, :]).reshape(3, 16, C)
             out[(2 * z + lev + 1) % 6, 0:3] = grid[:, 0:12, :].astype(BF16)
 
-    to_left.wait_send()
-    to_right.wait_send()
+    along(0, left).wait_send()
+    along(1, right).wait_send()
     regions.wait_send()
 
     @pl.when(has_above)
     def _():
-        up_left.wait_send()
-        up_right.wait_send()
+        for side, (far, col) in enumerate(sides):
+            pl.when(far)(corner(side, m_lat, la - 1, col).wait_send)
         up.wait_send()
 
     @pl.when(has_below)
     def _():
-        down.wait_send()
+        for side, (far, col) in enumerate(sides):
+            pl.when(jnp.logical_not(far))(corner(side, r_lat, la, col).wait_send)
+        down(0).wait_send()
+        down(1).wait_send()
 
 
 def shards(n_lat, n_lon, *args):
@@ -473,35 +525,36 @@
         pltpu.VMEM((2, 128, C), F32),
         packed(LON, 2),
         packed(LAT, 2),
-        packed(RET),
+        packed(LAT, 2),
         packed(LON, 2),
         packed(LAT, 2),
         packed(LAT, 2),
-        packed(RET),
+        packed(LAT, 2),
         pltpu.VMEM((2, 3 * BC, C), F32),
         pltpu.VMEM((2, 3 * BC, C), F32),
         pltpu.VMEM((2, 3 * BC, C), F32),
-        pltpu.VMEM((2, 3 * BC, C), BF16),
+        pltpu.VMEM((3 * BC, C), BF16),
         pltpu.VMEM((2, 128, C), BF16),
-        pltpu.VMEM((2, 128, C), BF16),
-        pltpu.VMEM((2, 3 * BC, C), F32),
-        pltpu.VMEM((2, 3 * BC, C), F32),
+        pltpu.VMEM((128, C), BF16),
+        pltpu.VMEM((3 * BC, C), F32),
+        pltpu.VMEM((3 * BC, C), F32),
         pltpu.VMEM((2, 128, C), F32),
         pltpu.VMEM((2, 128, C), F32),
         pltpu.VMEM((2, 128, C), F32),
-        pltpu.VMEM((2, 128, C), F32),
-        pltpu.VMEM((2, 128, C), F32),
+        pltpu.VMEM((128, C), F32),
+        pltpu.VMEM((128, C), F32),
         pltpu.VMEM((2, HEADS * NB, 2 * NB), F32),
         pltpu.VMEM((2, HEADS * 2 * NC, 4 * NC), F32),
         pltpu.VMEM((16, 128), F32),
-        pltpu.VMEM((3, 2, BC, C), F32),
-        pltpu.VMEM((6 * NC, C), F32),
-        pltpu.VMEM((6 * NC, C), BF16),
-        pltpu.VMEM((2 * BC, C), BF16),
+        pltpu.VMEM((3 * BC, C), F32),
+        pltpu.VMEM((128, C), F32),
+        pltpu.VMEM((2, 128, C), BF16),
+        pltpu.VMEM((2, 3 * BC, C), BF16),
         pltpu.VMEM((6 * NC, C), BF16),
         pltpu.SemaphoreType.DMA((7,)),
-        pltpu.SemaphoreType.DMA((7,)),
-        pltpu.SemaphoreType.DMA((7,)),
+        pltpu.SemaphoreType.DMA((8,)),
+        pltpu.SemaphoreType.DMA((8,)),
+        pltpu.SemaphoreType.REGULAR,
     ]
     return pl.pallas_call(
         functools.partial(kernel, n_lat, n_lon),

time: 28.2 us -> 25.2 us (0.89)
  the two profiles are of different devices: /device:TPU:256 before, /device:TPU:255 now
where the time goes in v3:
time: 25.2 us; the launch traced here: 25 us
  Pallas kernels  24.2 us (96%)
  local copies, waits for them, and re-layouts  0.82 us (3%)
    pallas_call x1, Pallas kernels, shards(): pl.pallas_call(functools.partial(kernel, n_lat, n_lon), out_shape=pltpu.V...  24.2 us
    unnamed x1, local copies, waits for them, and re-layouts  0.82 us

profile of v3, /device:TPU:255, one launch (start us, length us, event | category | flops | bytes accessed | tf_op | source)
XLA Modules:
  0.0 25.0 jit_solution(13942818902541876498)
XLA Ops:
  0.0 24.2 %shard_map.73 = bf16[6,12,12,192]{3,2,1,0:T(8,128)(2,1)S(1)} custom-call(bf16[6,12,12,192]{3,2,1,0:T(8,128)(2,1)} %state.1, bf16[2,6,144,144]{3,2,1,0:T(8,128)(2,1)} %attn_bias.1, s32[12,12]{1,0:T(8,128)} %region_ids.1, bf16[192,576]{1,0:T(8,128)(2,1)} %w_qkv.1, bf16[192,192]{1,0:T(8,128)(2,1)} %w_out.1, bf16[192,768]{1,0:T(8,128)(2,1)} %w_up.1, ...), custom_call_target="tpu_custom_call" | custom-call | tf_op jit(solution)/shard_map/pallas_call | solution.py:559
  24.2 0.8 %copy.9 = bf16[6,12,12,192]{3,2,1,0:T(8,128)(2,1)} copy(bf16[6,12,12,192]{3,2,1,0:T(8,128)(2,1)S(1)} %shard_map.73) | data formatting | bytes 663552

commit v4 on v3

--- a/solution.py
+++ b/solution.py
@@ -21,8 +21,8 @@
 F32 = jnp.float32
 BF16 = jnp.bfloat16
 
-LON = (3 * BC, 176, 160)
-LAT = (128, 64, 64)
+FULL = (224, 112, 112)
+HALVED = (128, 64, 64)
 
 
 def dot(a, b):
@@ -137,25 +137,28 @@
     dst[second : second + rest, 128:192] = tail[:, 64:128]
 
 
-def attend(q, k, v, bias):
-    n = q.shape[0]
+def attend(windows):
+    n = windows[0][0].shape[0]
     head = iota((1, C), 1) >> 5
-    stacked = jnp.concatenate([jnp.where(head == h, q, 0.0) for h in range(HEADS)], axis=0)
-    scores = dot_nt(stacked.astype(BF16), k) * SCALE + bias
-    top = jnp.max(scores, axis=-1, keepdims=True)
-    weights = jnp.exp(scores - top)
-    total = jnp.sum(weights, axis=-1, keepdims=True)
-    mixed = dot(weights.astype(BF16), v) * (1.0 / total)
-    out = jnp.where(head == 0, mixed[0:n], 0.0)
-    for h in range(1, HEADS):
-        out = jnp.where(head == h, mixed[h * n : (h + 1) * n], out)
-    return out
+    stacked = [jnp.concatenate([jnp.where(head == h, q, 0.0) for h in range(HEADS)], axis=0).astype(BF16) for q, *_ in windows]
+    scores = [dot_nt(s, k) * SCALE + bias for s, (_, k, _, bias) in zip(stacked, windows)]
+    tops = [jnp.max(s, axis=-1, keepdims=True) for s in scores]
+    weights = [jnp.exp(s - t) for s, t in zip(scores, tops)]
+    totals = [1.0 / jnp.sum(w, axis=-1, keepdims=True) for w in weights]
+    outs = []
+    for w, t, (_, _, v, _) in zip(weights, totals, windows):
+        mixed = dot(w.astype(BF16), v) * t
+        out = jnp.where(head == 0, mixed[0:n], 0.0)
+        for h in range(1, HEADS):
+            out = jnp.where(head == h, mixed[h * n : (h + 1) * n], out)
+        outs.append(out)
+    return outs
 
 
 def feed_forward(residual, w_up, w_down):
     normed = layer_norm(residual).astype(BF16)
     hidden = jax.nn.gelu(dot(normed, w_up)).astype(BF16)
-    return residual + dot_nt(hidden, w_down)
+    return residual + dot(hidden, w_down)
 
 
 def kernel(
@@ -180,25 +183,29 @@
     wo_v,
     wu_v,
     wd_v,
+    wd_t,
     xp,
     st,
-    normed,
+    normed_b,
+    normed_c,
     normed_a,
-    m_lon,
+    m_b,
+    m_c,
     m_lat,
     m_ret,
-    r_lon,
+    r_b,
+    r_c,
     r_lat,
     r_diag,
     r_ret,
-    own_q,
-    own_k,
-    own_v,
-    halo_x,
+    own_b,
+    own_c,
+    halo_bx,
+    halo_cx,
     lat_x,
     diag_x,
-    halo_k,
-    halo_v,
+    halo_b,
+    halo_c,
     lat_q,
     lat_k,
     lat_v,
@@ -263,7 +270,8 @@
         load.start()
 
     xp[...] = jnp.zeros_like(xp)
-    normed_a[...] = jnp.zeros_like(normed_a)
+    for ref in (normed_a, normed_b, normed_c):
+        ref[...] = jnp.zeros_like(ref)
     mix_ret[...] = jnp.zeros_like(mix_ret)
     gathers = [gather_of(0), gather_of(1)]
     loads[0].wait()
@@ -275,11 +283,13 @@
             x = dot(gathers[side], tokens)
             st[side, z] = x
             x = layer_norm(x)
-            normed[side, z * BC : (z + 1) * BC, :] = x[0:BC]
+            normed_b[side, z * NB : (z + 1) * NB, :] = x[0:NB]
+            normed_c[side, z * NC : (z + 1) * NC, :] = x[NB:BC]
             normed_a[side, z * NC : (z + 1) * NC, :] = x[BC : BC + NC]
     for side in range(2):
-        pack(m_lon.at[side], normed[side], LON)
-        pack(m_lat.at[side], normed_a[side], LAT)
+        pack(m_b.at[side], normed_b[side], FULL)
+        pack(m_c.at[side], normed_c[side], HALVED)
+        pack(m_lat.at[side], normed_a[side], HALVED)
 
     def remote(src, dst, i, device):
         return pltpu.make_async_remote_copy(
@@ -291,8 +301,11 @@
             device_id_type=MESH,
         )
 
-    def along(side, col):
-        return remote(m_lon.at[side], r_lon.at[1 - side], 1 - side, (la, col))
+    def along_b(side, col):
+        return remote(m_b.at[side], r_b.at[1 - side], 1 - side, (la, col))
+
+    def along_c(side, col):
+        return remote(m_c.at[side], r_c.at[1 - side], 9 - side, (la, col))
 
     def corner(side, source, row, col):
         return remote(source.at[side], r_diag.at[1 - side], 3 - side, (row, col))
@@ -319,14 +332,16 @@
         pl.when(has_above)(up.start)
         pl.when(jnp.logical_not(far_right))(regions.start)
         for side, (far, col) in enumerate(sides):
-            pl.when(jnp.logical_not(far))(along(side, col).start)
+            pl.when(jnp.logical_not(far))(along_b(side, col).start)
+            pl.when(jnp.logical_not(far))(along_c(side, col).start)
 
     def send_far():
         pl.semaphore_wait(barrier, 1 + rows)
         pl.when(far_right)(regions.start)
         for side, (far, col) in enumerate(sides):
             pl.when(far & has_above)(corner(side, m_lat, la - 1, col).start)
-            pl.when(far)(along(side, col).start)
+            pl.when(far)(along_c(side, col).start)
+            pl.when(far)(along_b(side, col).start)
 
     def prepare():
         loads[1].wait()
@@ -334,10 +349,10 @@
         wk[...] = wqkv_v[:, 192:384]
         wv[...] = wqkv_v[:, 384:576]
         for side in range(2):
-            x = normed[side].astype(BF16)
-            own_q[side] = dot(x, wq[...])
-            own_k[side] = dot(x, wk[...])
-            own_v[side] = dot(x, wv[...])
+            for own, normed in ((own_b, normed_b), (own_c, normed_c)):
+                x = normed[side].astype(BF16)
+                for i, w in enumerate((wq, wk, wv)):
+                    own[side, i] = dot(x, w[...])
         loads[2].wait()
         for band, (store, n, m) in enumerate(((bias_b, NB, 2 * NB), (bias_c, 2 * NC, 4 * NC))):
             for side in range(2):
@@ -349,6 +364,8 @@
                 store[side] = dot_nt(rows, select)
         loads[3].wait()
         apply_mask(1, region)
+        loads[6].wait()
+        wd_t[...] = wd_v[...].T
 
     def apply_mask(side, source):
         labels[...] = jnp.zeros_like(labels)
@@ -380,80 +397,106 @@
 
     lax.fori_loop(0, 3, start, 0)
 
-    @pl.when(has_below)
-    def _():
-        up.wait_recv()
-        for side, (far, col) in enumerate(sides):
-            pl.when(jnp.logical_not(far))(corner(side, r_lat, la, col).start)
-
-    @pl.when(jnp.logical_not(has_below))
-    def _():
-        r_lat[...] = jnp.zeros_like(r_lat)
-        r_diag[...] = jnp.zeros_like(r_diag)
-
-    for side in range(2):
-        unpack(lat_x.at[side], r_lat.at[side], LAT)
-        x = lat_x[side]
-        lat_q[side] = dot(x, wq[...])
-        lat_k[side] = dot(x, wk[...])
-        lat_v[side] = dot(x, wv[...])
     loads[4].wait()
     loads[5].wait()
-    loads[6].wait()
-
-    def window_column(i, carry):
-        side = jnp.where(far_left, 1 - i, i)
-
+
+    def down(side):
+        return remote(m_ret.at[side], r_ret.at[side], 6 + side, (la + 1, lo))
+
+    def mask(side):
         @pl.when(side == 0)
         def _():
             regions.wait_recv()
             apply_mask(0, region_left)
 
-        along(1 - side, left).wait_recv()
-        unpack(halo_x, r_lon.at[side], LON)
-        x = halo_x[...]
-        halo_k[...] = dot(x, wk[...])
-        halo_v[...] = dot(x, wv[...])
-
+    def halo(copy, x_ref, buf, keys_values, form):
+        copy.wait_recv()
+        unpack(x_ref, buf, form)
+        x = x_ref[...]
+        keys_values[0] = dot(x, wk[...])
+        keys_values[1] = dot(x, wv[...])
+
+    def rows_below():
         @pl.when(has_below)
         def _():
+            up.wait_recv()
+            for side, (far, col) in enumerate(sides):
+                pl.when(jnp.logical_not(far))(corner(side, r_lat, la, col).start)
+
+        @pl.when(jnp.logical_not(has_below))
+        def _():
+            r_lat[...] = jnp.zeros_like(r_lat)
+            r_diag[...] = jnp.zeros_like(r_diag)
+
+        for side in range(2):
+            unpack(lat_x.at[side], r_lat.at[side], HALVED)
+            x = lat_x[side]
+            lat_q[side] = dot(x, wq[...])
+            lat_k[side] = dot(x, wk[...])
+            lat_v[side] = dot(x, wv[...])
+
+    def windows_c(side):
+        @pl.when(has_below)
+        def _():
             corner(1 - side, r_lat, la, left).wait_recv()
 
-        unpack(diag_x, r_diag.at[side], LAT)
+        halo(along_c(1 - side, left), halo_cx, r_c.at[side], halo_c, HALVED)
+        unpack(diag_x, r_diag.at[side], HALVED)
         x = diag_x[...]
         diag_k[...] = dot(x, wk[...])
         diag_v[...] = dot(x, wv[...])
-
+        windows = []
         for z in range(3):
             a = pl.ds(z * NC, NC)
-            c = pl.ds(z * BC + NB, NC)
-            q = jnp.concatenate([own_q[side, c], lat_q[side, a]], axis=0)
-            k = jnp.concatenate([own_k[side, c], lat_k[side, a], halo_k[c], diag_k[a]], axis=0)
-            v = jnp.concatenate([own_v[side, c], lat_v[side, a], halo_v[c], diag_v[a]], axis=0)
-            context = attend(q, k.astype(BF16), v.astype(BF16), bias_c[side])
-            mixed = dot(context.astype(BF16), wo_v[...]).astype(BF16).astype(F32)
-            mix[z * BC + NB : (z + 1) * BC, :] = mixed[0:NC]
-            mix_ret[z * NC : (z + 1) * NC, :] = mixed[NC : 2 * NC]
-        pack(m_ret.at[side], mix_ret[...], LAT)
+            q = jnp.concatenate([own_c[side, 0, a], lat_q[side, a]], axis=0)
+            k = jnp.concatenate([own_c[side, 1, a], lat_k[side, a], halo_c[0, a], diag_k[a]], axis=0)
+            v = jnp.concatenate([own_c[side, 2, a], lat_v[side, a], halo_c[1, a], diag_v[a]], axis=0)
+            windows.append((q, k.astype(BF16), v.astype(BF16), bias_c[side]))
+        context = jnp.concatenate(attend(windows), axis=0)
+        mixed = dot(context.astype(BF16), wo_v[...]).astype(BF16).astype(F32)
+        for z in range(3):
+            at = z * 2 * NC
+            mix[side, z * BC + NB : (z + 1) * BC, :] = mixed[at : at + NC]
+            mix_ret[z * NC : (z + 1) * NC, :] = mixed[at + NC : at + 2 * NC]
+        pack(m_ret.at[side], mix_ret[...], HALVED)
 
         @pl.when(has_below)
         def _():
             down(side).start()
 
+    def windows_b(side):
+        halo(along_b(1 - side, left), halo_bx, r_b.at[side], halo_b, FULL)
+        windows = []
         for z in range(3):
-            b = pl.ds(z * BC, NB)
-            k = jnp.concatenate([own_k[side, b], halo_k[b]], axis=0)
-            v = jnp.concatenate([own_v[side, b], halo_v[b]], axis=0)
-            context = attend(own_q[side, b], k.astype(BF16), v.astype(BF16), bias_b[side])
-            mix[z * BC : z * BC + NB, :] = dot(context.astype(BF16), wo_v[...]).astype(BF16).astype(F32)
-        residual = jnp.concatenate([st[side, z, 0:BC] for z in range(3)], axis=0) + mix[...]
-        out_bc[side] = feed_forward(residual, wu_v[...], wd_v[...]).astype(BF16)
+            b = pl.ds(z * NB, NB)
+            k = jnp.concatenate([own_b[side, 1, b], halo_b[0, b]], axis=0)
+            v = jnp.concatenate([own_b[side, 2, b], halo_b[1, b]], axis=0)
+            windows.append((own_b[side, 0, b], k.astype(BF16), v.astype(BF16), bias_b[side]))
+        context = jnp.concatenate(attend(windows), axis=0)
+        mixed = dot(context.astype(BF16), wo_v[...]).astype(BF16).astype(F32)
+        for z in range(3):
+            mix[side, z * BC : z * BC + NB, :] = mixed[z * NB : (z + 1) * NB]
+
+    def feed(side):
+        residual = jnp.concatenate([st[side, z, 0:BC] for z in range(3)], axis=0) + mix[side]
+        out_bc[side] = feed_forward(residual, wu_v[...], wd_t[...]).astype(BF16)
+
+    late = lax.rem(la, 4) == 3
+    first_right = far_left | end_on_left
+
+    def task(step, carry):
+        second = (step >= 3) & (step != 4) | jnp.where(late, step == 2, step == 4)
+        second = jnp.where(second, 1, 0)
+        side = jnp.where(first_right, 1 - second, second)
+        second_c = jnp.where(late, 2, 3)
+        pl.when((step == 0) | (step == second_c))(functools.partial(mask, side))
+        pl.when(step == 1)(rows_below)
+        pl.when((step == 1) | (step == second_c))(functools.partial(windows_c, side))
+        pl.when((step == 0) | (step == second_c + 1))(functools.partial(windows_b, side))
+        pl.when((step == 5) | (step == jnp.where(late, 4, 2)))(functools.partial(feed, side))
         return carry
 
-    def down(side):
-        return remote(m_ret.at[side], r_ret.at[side], 6 + side, (la + 1, lo))
-
-    lax.fori_loop(0, 2, window_column, 0)
+    lax.fori_loop(0, 6, task, 0)
 
     for lev in range(2):
         scatter = scatter_of(lev, 9, True)
@@ -472,19 +515,20 @@
         r_ret[...] = jnp.zeros_like(r_ret)
 
     for side in range(2):
-        unpack(ret_x.at[side], r_ret.at[side], LAT)
+        unpack(ret_x.at[side], r_ret.at[side], HALVED)
     residual = [
         st[side, z, BC : BC + NC] + ret_x[side, z * NC : (z + 1) * NC, :].astype(F32) for z in range(3) for side in range(2)
     ]
-    out_a[...] = feed_forward(jnp.concatenate(residual, axis=0), wu_v[...], wd_v[...]).astype(BF16)
+    out_a[...] = feed_forward(jnp.concatenate(residual, axis=0), wu_v[...], wd_t[...]).astype(BF16)
     for lev in range(2):
         scatter = scatter_of(lev, 3, False)
         for z in range(3):
             grid = dot(scatter, out_a[z * 2 * NC : (z + 1) * 2 * NC, :]).reshape(3, 16, C)
             out[(2 * z + lev + 1) % 6, 0:3] = grid[:, 0:12, :].astype(BF16)
 
-    along(0, left).wait_send()
-    along(1, right).wait_send()
+    for copy in (along_b, along_c):
+        copy(0, left).wait_send()
+        copy(1, right).wait_send()
     regions.wait_send()
 
     @pl.when(has_above)
@@ -519,25 +563,29 @@
         pltpu.VMEM((C, C), BF16),
         pltpu.VMEM((C, FF), BF16),
         pltpu.VMEM((C, FF), BF16),
+        pltpu.VMEM((FF, C), BF16),
         pltpu.VMEM((6, 12, 16, C), F32),
         pltpu.VMEM((2, 3, BC + NC, C), F32),
-        pltpu.VMEM((2, 3 * BC, C), F32),
+        pltpu.VMEM((2, 224, C), F32),
         pltpu.VMEM((2, 128, C), F32),
-        packed(LON, 2),
-        packed(LAT, 2),
-        packed(LAT, 2),
-        packed(LON, 2),
-        packed(LAT, 2),
-        packed(LAT, 2),
-        packed(LAT, 2),
-        pltpu.VMEM((2, 3 * BC, C), F32),
-        pltpu.VMEM((2, 3 * BC, C), F32),
-        pltpu.VMEM((2, 3 * BC, C), F32),
-        pltpu.VMEM((3 * BC, C), BF16),
+        pltpu.VMEM((2, 128, C), F32),
+        packed(FULL, 2),
+        packed(HALVED, 2),
+        packed(HALVED, 2),
+        packed(HALVED, 2),
+        packed(FULL, 2),
+        packed(HALVED, 2),
+        packed(HALVED, 2),
+        packed(HALVED, 2),
+        packed(HALVED, 2),
+        pltpu.VMEM((2, 3, 224, C), F32),
+        pltpu.VMEM((2, 3, 128, C), F32),
+        pltpu.VMEM((224, C), BF16),
+        pltpu.VMEM((128, C), BF16),
         pltpu.VMEM((2, 128, C), BF16),
         pltpu.VMEM((128, C), BF16),
-        pltpu.VMEM((3 * BC, C), F32),
-        pltpu.VMEM((3 * BC, C), F32),
+        pltpu.VMEM((2, 224, C), F32),
+        pltpu.VMEM((2, 128, C), F32),
         pltpu.VMEM((2, 128, C), F32),
         pltpu.VMEM((2, 128, C), F32),
         pltpu.VMEM((2, 128, C), F32),
@@ -546,14 +594,14 @@
         pltpu.VMEM((2, HEADS * NB, 2 * NB), F32),
         pltpu.VMEM((2, HEADS * 2 * NC, 4 * NC), F32),
         pltpu.VMEM((16, 128), F32),
-        pltpu.VMEM((3 * BC, C), F32),
+        pltpu.VMEM((2, 3 * BC, C), F32),
         pltpu.VMEM((128, C), F32),
         pltpu.VMEM((2, 128, C), BF16),
         pltpu.VMEM((2, 3 * BC, C), BF16),
         pltpu.VMEM((6 * NC, C), BF16),
         pltpu.SemaphoreType.DMA((7,)),
-        pltpu.SemaphoreType.DMA((8,)),
-        pltpu.SemaphoreType.DMA((8,)),
+        pltpu.SemaphoreType.DMA((10,)),
+        pltpu.SemaphoreType.DMA((10,)),
         pltpu.SemaphoreType.REGULAR,
     ]
     return pl.pallas_call(

time: 25.2 us -> 23.4 us (0.929)
  the two profiles are of different devices: /device:TPU:255 before, /device:TPU:8 now
where the time goes in v4:
time: 23.4 us; the launch traced here: 23.3 us
  Pallas kernels  22.4 us (96%)
  local copies, waits for them, and re-layouts  0.82 us (4%)
    pallas_call x1, Pallas kernels, shards(): pl.pallas_call(functools.partial(kernel, n_lat, n_lon), out_shape=pltpu.V...  22.4 us
    unnamed x1, local copies, waits for them, and re-layouts  0.82 us

profile of v4, /device:TPU:8, one launch (start us, length us, event | category | flops | bytes accessed | tf_op | source)
XLA Modules:
  0.0 23.3 jit_solution(16733854605917670473)
XLA Ops:
  0.0 22.4 %shard_map.73 = bf16[6,12,12,192]{3,2,1,0:T(8,128)(2,1)S(1)} custom-call(bf16[6,12,12,192]{3,2,1,0:T(8,128)(2,1)} %state.1, bf16[2,6,144,144]{3,2,1,0:T(8,128)(2,1)} %attn_bias.1, s32[12,12]{1,0:T(8,128)} %region_ids.1, bf16[192,576]{1,0:T(8,128)(2,1)} %w_qkv.1, bf16[192,192]{1,0:T(8,128)(2,1)} %w_out.1, bf16[192,768]{1,0:T(8,128)(2,1)} %w_up.1, ...), custom_call_target="tpu_custom_call" | custom-call | tf_op jit(solution)/shard_map/pallas_call | solution.py:607
  22.4 0.8 %copy.9 = bf16[6,12,12,192]{3,2,1,0:T(8,128)(2,1)} copy(bf16[6,12,12,192]{3,2,1,0:T(8,128)(2,1)S(1)} %shard_map.73) | data formatting | bytes 663552

commit v5 on v4

--- a/solution.py
+++ b/solution.py
@@ -83,18 +83,13 @@
     return one_hot(iota((BC + NC, 384), 1) == source)
 
 
-def scatter_of(lev, rows, full):
+def scatter_of(lev, full):
+    rows, width = (6, NB) if full else (3, NC)
     d = iota((rows * 16, 1), 0)
     row, col = d >> 4, d & 15
     side = jnp.where(col >= HALF, 1, 0)
-    cc = col - HALF * side
-    if full:
-        at = jnp.where(row < 6, lev * 36 + row * 6 + cc, NB + lev * 18 + (row - 6) * 6 + cc)
-        width = BC
-    else:
-        at = lev * 18 + row * 6 + cc
-        width = NC
-    source = jnp.where(col < 12, side * width + at, -1)
+    source = side * width + lev * rows * HALF + row * HALF + col - HALF * side
+    source = jnp.where(col < 12, source, -1)
     return one_hot(iota((rows * 16, 2 * width), 1) == source)
 
 
@@ -214,11 +209,11 @@
     bias_b,
     bias_c,
     labels,
-    mix,
+    mix_b,
+    mix_c,
     mix_ret,
     ret_x,
-    out_bc,
-    out_a,
+    out_b,
     load_sem,
     send_sem,
     recv_sem,
@@ -356,12 +351,14 @@
         loads[2].wait()
         for band, (store, n, m) in enumerate(((bias_b, NB, 2 * NB), (bias_c, 2 * NC, 4 * NC))):
             for side in range(2):
-                lev, row, col, valid = key_place(iota((m, 1), 0), band, side)
+                lev, row, col, valid = key_place(iota((n, 1), 0), band, side)
                 at = jnp.where(valid, lev * 72 + row * 12 + col, -1)
-                select = one_hot(iota((m, 144), 1) == at)
-                rows = [dot(select[0:n], bias_in[band, h]) for h in range(HEADS)]
+                select = one_hot(iota((n, 144), 1) == at)
+                rows = [dot(select, bias_in[band, h]) for h in range(HEADS)]
                 rows = jnp.concatenate(rows, axis=0).astype(BF16)
-                store[side] = dot_nt(rows, select)
+                lev, row, col, valid = key_place(iota((1, m), 1), band, side)
+                at = jnp.where(valid, lev * 72 + row * 12 + col, -1)
+                store[side] = dot(rows, one_hot(iota((144, m), 0) == at))
         loads[3].wait()
         apply_mask(1, region)
         loads[6].wait()
@@ -403,11 +400,9 @@
     def down(side):
         return remote(m_ret.at[side], r_ret.at[side], 6 + side, (la + 1, lo))
 
-    def mask(side):
-        @pl.when(side == 0)
-        def _():
-            regions.wait_recv()
-            apply_mask(0, region_left)
+    def mask():
+        regions.wait_recv()
+        apply_mask(0, region_left)
 
     def halo(copy, x_ref, buf, keys_values, form):
         copy.wait_recv()
@@ -456,7 +451,7 @@
         mixed = dot(context.astype(BF16), wo_v[...]).astype(BF16).astype(F32)
         for z in range(3):
             at = z * 2 * NC
-            mix[side, z * BC + NB : (z + 1) * BC, :] = mixed[at : at + NC]
+            mix_c[side, z * NC : (z + 1) * NC, :] = mixed[at : at + NC]
             mix_ret[z * NC : (z + 1) * NC, :] = mixed[at + NC : at + 2 * NC]
         pack(m_ret.at[side], mix_ret[...], HALVED)
 
@@ -475,35 +470,54 @@
         context = jnp.concatenate(attend(windows), axis=0)
         mixed = dot(context.astype(BF16), wo_v[...]).astype(BF16).astype(F32)
         for z in range(3):
-            mix[side, z * BC : z * BC + NB, :] = mixed[z * NB : (z + 1) * NB]
-
-    def feed(side):
-        residual = jnp.concatenate([st[side, z, 0:BC] for z in range(3)], axis=0) + mix[side]
-        out_bc[side] = feed_forward(residual, wu_v[...], wd_t[...]).astype(BF16)
+            mix_b[side, z * NB : (z + 1) * NB, :] = mixed[z * NB : (z + 1) * NB]
+
+    def feed_b(side):
+        residual = jnp.concatenate([st[side, z, 0:NB] for z in range(3)], axis=0) + mix_b[side]
+        out_b[side] = feed_forward(residual, wu_v[...], wd_t[...])
 
     late = lax.rem(la, 4) == 3
+    inner = late & jnp.logical_not(end)
     first_right = far_left | end_on_left
+    first = jnp.where(first_right, 1, 0)
+    at_c = (jnp.where(inner, 4, jnp.where(late, 2, 1)), jnp.where(inner, 5, 3))
+    at_b = (0, jnp.where(inner, 1, 4))
+    at_feed = jnp.where(late & end, 1, jnp.where(inner, 3, 2))
 
     def task(step, carry):
-        second = (step >= 3) & (step != 4) | jnp.where(late, step == 2, step == 4)
-        second = jnp.where(second, 1, 0)
-        side = jnp.where(first_right, 1 - second, second)
-        second_c = jnp.where(late, 2, 3)
-        pl.when((step == 0) | (step == second_c))(functools.partial(mask, side))
-        pl.when(step == 1)(rows_below)
-        pl.when((step == 1) | (step == second_c))(functools.partial(windows_c, side))
-        pl.when((step == 0) | (step == second_c + 1))(functools.partial(windows_b, side))
-        pl.when((step == 5) | (step == jnp.where(late, 4, 2)))(functools.partial(feed, side))
+        second = (step == at_c[1]) | (step == at_b[1])
+        side = jnp.where(second, 1 - first, first)
+        pl.when(step == jnp.where(first_right, jnp.where(inner, 1, 2), 0))(mask)
+        pl.when(step == jnp.where(late, at_c[0], 0))(rows_below)
+        pl.when((step == at_c[0]) | (step == at_c[1]))(functools.partial(windows_c, side))
+        pl.when((step == at_b[0]) | (step == at_b[1]))(functools.partial(windows_b, side))
+        pl.when(step == at_feed)(functools.partial(feed_b, side))
         return carry
 
     lax.fori_loop(0, 6, task, 0)
 
+    def put(lev, z, row, grid):
+        rows = grid.shape[0] // 16
+        out[(2 * z + lev + 1) % 6, row : row + rows] = grid.reshape(rows, 16, C)[:, 0:12, :].astype(BF16)
+
+    def scatter_rows(done, row):
+        for lev in range(2):
+            scatter = scatter_of(lev, False)
+            for z in range(3):
+                put(lev, z, row, dot(scatter, done[z * 2 * NC : (z + 1) * 2 * NC].astype(BF16)))
+
+    pairs = [(z, side) for z in range(3) for side in range(2)]
+    residual = [st[1 - first, z, 0:NB] + mix_b[1 - first, z * NB : (z + 1) * NB, :] for z in range(3)]
+    residual += [st[side, z, NB:BC] + mix_c[side, z * NC : (z + 1) * NC, :] for z, side in pairs]
+    done = feed_forward(jnp.concatenate(residual, axis=0), wu_v[...], wd_t[...])
+    out_b[1 - first] = done[0 : 3 * NB]
+    scatter_rows(done[3 * NB :], 9)
     for lev in range(2):
-        scatter = scatter_of(lev, 9, True)
+        scatter = scatter_of(lev, True)
         for z in range(3):
-            part = pl.ds(z * BC, BC)
-            grid = dot(scatter, jnp.concatenate([out_bc[0, part], out_bc[1, part]], axis=0)).reshape(9, 16, C)
-            out[(2 * z + lev + 1) % 6, 3:12] = grid[:, 0:12, :].astype(BF16)
+            part = pl.ds(z * NB, NB)
+            tokens = jnp.concatenate([out_b[0, part], out_b[1, part]], axis=0).astype(BF16)
+            put(lev, z, 3, dot(scatter, tokens))
 
     @pl.when(has_above)
     def _():
@@ -516,15 +530,8 @@
 
     for side in range(2):
         unpack(ret_x.at[side], r_ret.at[side], HALVED)
-    residual = [
-        st[side, z, BC : BC + NC] + ret_x[side, z * NC : (z + 1) * NC, :].astype(F32) for z in range(3) for side in range(2)
-    ]
-    out_a[...] = feed_forward(jnp.concatenate(residual, axis=0), wu_v[...], wd_t[...]).astype(BF16)
-    for lev in range(2):
-        scatter = scatter_of(lev, 3, False)
-        for z in range(3):
-            grid = dot(scatter, out_a[z * 2 * NC : (z + 1) * 2 * NC, :]).reshape(3, 16, C)
-            out[(2 * z + lev + 1) % 6, 0:3] = grid[:, 0:12, :].astype(BF16)
+    residual = [st[side, z, BC : BC + NC] + ret_x[side, z * NC : (z + 1) * NC, :].astype(F32) for z, side in pairs]
+    scatter_rows(feed_forward(jnp.concatenate(residual, axis=0), wu_v[...], wd_t[...]), 0)
 
     for copy in (along_b, along_c):
         copy(0, left).wait_send()
@@ -594,11 +601,11 @@
         pltpu.VMEM((2, HEADS * NB, 2 * NB), F32),
         pltpu.VMEM((2, HEADS * 2 * NC, 4 * NC), F32),
         pltpu.VMEM((16, 128), F32),
-        pltpu.VMEM((2, 3 * BC, C), F32),
+        pltpu.VMEM((2, 3 * NB, C), F32),
+        pltpu.VMEM((2, 3 * NC, C), F32),
         pltpu.VMEM((128, C), F32),
         pltpu.VMEM((2, 128, C), BF16),
-        pltpu.VMEM((2, 3 * BC, C), BF16),
-        pltpu.VMEM((6 * NC, C), BF16),
+        pltpu.VMEM((2, 3 * NB, C), F32),
         pltpu.SemaphoreType.DMA((7,)),
         pltpu.SemaphoreType.DMA((10,)),
         pltpu.SemaphoreType.DMA((10,)),

time: 23.4 us -> 23.4 us (level)
  no operation moved by 1% of the time
where the time goes in v5:
time: 23.4 us; the launch traced here: 23.3 us
  Pallas kernels  22.4 us (96%)
  local copies, waits for them, and re-layouts  0.82 us (4%)
    pallas_call x1, Pallas kernels, shards(): pl.pallas_call(functools.partial(kernel, n_lat, n_lon), out_shape=pltpu.V...  22.4 us
    unnamed x1, local copies, waits for them, and re-layouts  0.82 us

profile of v5, /device:TPU:8, one launch (start us, length us, event | category | flops | bytes accessed | tf_op | source)
XLA Modules:
  0.0 23.3 jit_solution(1563194162275785379)
XLA Ops:
  0.0 22.4 %shard_map.73 = bf16[6,12,12,192]{3,2,1,0:T(8,128)(2,1)S(1)} custom-call(bf16[6,12,12,192]{3,2,1,0:T(8,128)(2,1)} %state.1, bf16[2,6,144,144]{3,2,1,0:T(8,128)(2,1)} %attn_bias.1, s32[12,12]{1,0:T(8,128)} %region_ids.1, bf16[192,576]{1,0:T(8,128)(2,1)} %w_qkv.1, bf16[192,192]{1,0:T(8,128)(2,1)} %w_out.1, bf16[192,768]{1,0:T(8,128)(2,1)} %w_up.1, ...), custom_call_target="tpu_custom_call" | custom-call | tf_op jit(solution)/shard_map/pallas_call | solution.py:614
  22.5 0.8 %copy.9 = bf16[6,12,12,192]{3,2,1,0:T(8,128)(2,1)} copy(bf16[6,12,12,192]{3,2,1,0:T(8,128)(2,1)S(1)} %shard_map.73) | data formatting | bytes 663552

commit v6 on v5

--- a/solution.py
+++ b/solution.py
@@ -487,11 +487,11 @@
     def task(step, carry):
         second = (step == at_c[1]) | (step == at_b[1])
         side = jnp.where(second, 1 - first, first)
+        pl.when(step == at_feed)(functools.partial(feed_b, side))
         pl.when(step == jnp.where(first_right, jnp.where(inner, 1, 2), 0))(mask)
         pl.when(step == jnp.where(late, at_c[0], 0))(rows_below)
         pl.when((step == at_c[0]) | (step == at_c[1]))(functools.partial(windows_c, side))
         pl.when((step == at_b[0]) | (step == at_b[1]))(functools.partial(windows_b, side))
-        pl.when(step == at_feed)(functools.partial(feed_b, side))
         return carry
 
     lax.fori_loop(0, 6, task, 0)

time: 23.4 us -> 23.4 us (level)
  no operation moved by 1% of the time
where the time goes in v6:
time: 23.4 us; the launch traced here: 23.3 us
  Pallas kernels  22.4 us (96%)
  local copies, waits for them, and re-layouts  0.82 us (4%)
    pallas_call x1, Pallas kernels, shards(): pl.pallas_call(functools.partial(kernel, n_lat, n_lon), out_shape=pltpu.V...  22.4 us
    unnamed x1, local copies, waits for them, and re-layouts  0.82 us

profile of v6, /device:TPU:8, one launch (start us, length us, event | category | flops | bytes accessed | tf_op | source)
XLA Modules:
  0.0 23.3 jit_solution(6002105573076917074)
XLA Ops:
  0.0 22.4 %shard_map.73 = bf16[6,12,12,192]{3,2,1,0:T(8,128)(2,1)S(1)} custom-call(bf16[6,12,12,192]{3,2,1,0:T(8,128)(2,1)} %state.1, bf16[2,6,144,144]{3,2,1,0:T(8,128)(2,1)} %attn_bias.1, s32[12,12]{1,0:T(8,128)} %region_ids.1, bf16[192,576]{1,0:T(8,128)(2,1)} %w_qkv.1, bf16[192,192]{1,0:T(8,128)(2,1)} %w_out.1, bf16[192,768]{1,0:T(8,128)(2,1)} %w_up.1, ...), custom_call_target="tpu_custom_call" | custom-call | tf_op jit(solution)/shard_map/pallas_call | solution.py:614
  22.5 0.8 %copy.9 = bf16[6,12,12,192]{3,2,1,0:T(8,128)(2,1)} copy(bf16[6,12,12,192]{3,2,1,0:T(8,128)(2,1)S(1)} %shard_map.73) | data formatting | bytes 663552

commit v7 on v6

--- a/solution.py
+++ b/solution.py
@@ -482,7 +482,7 @@
     first = jnp.where(first_right, 1, 0)
     at_c = (jnp.where(inner, 4, jnp.where(late, 2, 1)), jnp.where(inner, 5, 3))
     at_b = (0, jnp.where(inner, 1, 4))
-    at_feed = jnp.where(late & end, 1, jnp.where(inner, 3, 2))
+    at_feed = jnp.where(late & end, 1, jnp.where(inner, 3, jnp.where(end & jnp.logical_not(has_above), 5, 2)))
 
     def task(step, carry):
         second = (step == at_c[1]) | (step == at_b[1])

time: 23.4 us -> 23.4 us (level)
  no operation moved by 1% of the time
where the time goes in v7:
time: 23.4 us; the launch traced here: 23.3 us
  Pallas kernels  22.4 us (96%)
  local copies, waits for them, and re-layouts  0.82 us (4%)
    pallas_call x1, Pallas kernels, shards(): pl.pallas_call(functools.partial(kernel, n_lat, n_lon), out_shape=pltpu.V...  22.4 us
    unnamed x1, local copies, waits for them, and re-layouts  0.82 us

profile of v7, /device:TPU:8, one launch (start us, length us, event | category | flops | bytes accessed | tf_op | source)
XLA Modules:
  0.0 23.3 jit_solution(13742625316341852958)
XLA Ops:
  0.0 22.4 %shard_map.73 = bf16[6,12,12,192]{3,2,1,0:T(8,128)(2,1)S(1)} custom-call(bf16[6,12,12,192]{3,2,1,0:T(8,128)(2,1)} %state.1, bf16[2,6,144,144]{3,2,1,0:T(8,128)(2,1)} %attn_bias.1, s32[12,12]{1,0:T(8,128)} %region_ids.1, bf16[192,576]{1,0:T(8,128)(2,1)} %w_qkv.1, bf16[192,192]{1,0:T(8,128)(2,1)} %w_out.1, bf16[192,768]{1,0:T(8,128)(2,1)} %w_up.1, ...), custom_call_target="tpu_custom_call" | custom-call | tf_op jit(solution)/shard_map/pallas_call | solution.py:614
  22.5 0.8 %copy.9 = bf16[6,12,12,192]{3,2,1,0:T(8,128)(2,1)} copy(bf16[6,12,12,192]{3,2,1,0:T(8,128)(2,1)S(1)} %shard_map.73) | data formatting | bytes 663552
